TPU v7x, 32 devices: a whole 2x2x4 slice. The times are simulated.
32 devices in a mesh: dp: 4 (over y, x), lat: 2 (over core), lon: 4 (over z).
Axes of the slice: x: 2, y: 2, z: 4, core: 2. Of those that a mesh axis runs over, the one named last changes fastest.
Arguments:
- tokens: bfloat16 [4, 3, 12, 48, 1024], P('dp', None, 'lat', 'lon'), may hold values from -6 to 6
- cotangent: bfloat16 [4, 3, 12, 48, 1024], P('dp', None, 'lat', 'lon'), may hold values from -6 to 6
- w_qkv: bfloat16 [2, 1024, 1536], P(None, ('lat', 'lon')), may hold values from -0.25 to 0.25
- w_out: bfloat16 [2, 512, 1024], P(None, ('lat', 'lon')), may hold values from -0.25 to 0.25
- gains: float32 [2, 1024], replicated, may hold values from 0.1 to 1.9
- tables: float32 [2, 8, 1265], replicated, may hold values from -8 to 304
Outputs:
- outputs: bfloat16 [4, 3, 12, 48, 1024], P('dp', None, 'lat', 'lon')
- grad_tokens: bfloat16 [4, 3, 12, 48, 1024], P('dp', None, 'lat', 'lon')
- grad_gains: float32 [2, 1024], replicated
- grad_tables: float32 [2, 8, 1265], replicated
All inputs are finite; a program needn't handle non-finite values.
Results may differ from a plain program's by a relative error of at most 0.033.
Values may be sent and summed in bfloat16 or wider, within the bound.
A program may use at most 128 MiB of HBM per device.

v0:
```python
import math

import jax
import jax.numpy as jnp
from jax import lax
from jax.sharding import PartitionSpec as P

HD = 64
H = 8
Z = 3
WH = 6
WW = 12
SH = 3
SW = 6


EPS = 1e-05


def passed_along(shard, axis, by):
    devices = lax.axis_size(axis)
    return lax.ppermute(shard, axis, [(i, (i + by) % devices) for i in range(devices)])


def offset_table():
    shape = (Z, WH, WW)
    level_ids = lax.broadcasted_iota(jnp.int32, shape, 0).reshape(-1)
    row_ids = lax.broadcasted_iota(jnp.int32, shape, 1).reshape(-1)
    col_ids = lax.broadcasted_iota(jnp.int32, shape, 2).reshape(-1)
    delta_z = level_ids[:, None] - level_ids[None, :]
    delta_y = row_ids[:, None] - row_ids[None, :]
    delta_x = col_ids[:, None] - col_ids[None, :]
    flat = (
        (delta_z + Z - 1) * (2 * WH - 1) * (2 * WW - 1)
        + (delta_y + WH - 1) * (2 * WW - 1)
        + delta_x
        + WW
        - 1
    )
    return flat.reshape(-1)


def to_windows(grid):
    time_count, levels, lat_rows, lon_cols, features = grid.shape
    grid = grid.reshape(time_count, levels, lat_rows // WH, WH, lon_cols // WW, WW, features)
    grid = grid.transpose(0, 2, 4, 1, 3, 5, 6)
    return grid.reshape(
        time_count * (lat_rows // WH) * (lon_cols // WW), levels * WH * WW, features
    )


def from_windows(windows, time_count, lat_rows, lon_cols):
    features = windows.shape[-1]
    grid = windows.reshape(time_count, lat_rows // WH, lon_cols // WW, Z, WH, WW, features)
    grid = grid.transpose(0, 3, 1, 4, 2, 5, 6)
    return grid.reshape(time_count, Z, lat_rows, lon_cols, features)


def region_pairs(region):
    labels = to_windows(region[None, :, :, :, None])[:, :, 0]
    return labels[:, :, None] == labels[:, None, :]


def expand_table(table, offsets):
    span = Z * WH * WW
    return table[:, offsets].reshape(H, span, span)


def fold_table(full, offsets):
    summed = full.reshape(H, -1)
    return (
        jnp.zeros((H, (2 * Z - 1) * (2 * WH - 1) * (2 * WW - 1)), jnp.float32)
        .at[:, offsets]
        .add(summed)
    )


def norm_parts(field, gain):
    values = field.astype(jnp.float32)
    centred = values - jnp.mean(values, -1, keepdims=True)
    inverse = lax.rsqrt(jnp.mean(centred * centred, -1, keepdims=True) + EPS)
    normed = centred * inverse
    return ((normed * gain).astype(jnp.bfloat16), normed, inverse)


def block_forward(field, gain, w_in, w_proj, bias, valid):
    time_count, levels, lat_rows, lon_cols, features = field.shape
    scale = HD ** (-0.5)
    normed_bf, normed, inverse = norm_parts(field, gain)
    mixed = jnp.dot(
        normed_bf.reshape(-1, features), w_in, preferred_element_type=jnp.float32
    ).astype(jnp.bfloat16)
    windows = to_windows(mixed.reshape(time_count, levels, lat_rows, lon_cols, 3 * H * HD))
    parts = windows.reshape(windows.shape[0], windows.shape[1], 3, H, HD)
    query, keys, values = (parts[:, :, 0], parts[:, :, 1], parts[:, :, 2])
    scores = (
        jnp.einsum("nihd,njhd->nhij", query, keys, preferred_element_type=jnp.float32) * scale
        + bias[None]
    )
    scores = jnp.where(valid[:, None], scores, -1e30)
    powers = jnp.exp(scores - jnp.max(scores, -1, keepdims=True))
    probs = (powers / jnp.sum(powers, -1, keepdims=True)).astype(jnp.bfloat16)
    context = jnp.einsum(
        "nhij,njhd->nihd", probs, values, preferred_element_type=jnp.float32
    ).astype(jnp.bfloat16)
    context = from_windows(
        context.reshape(windows.shape[0], windows.shape[1], H * HD), time_count, lat_rows, lon_cols
    )
    branch = jnp.dot(context.reshape(-1, H * HD), w_proj, preferred_element_type=jnp.float32)
    result = (field.astype(jnp.float32) + branch.reshape(field.shape)).astype(jnp.bfloat16)
    return (result, (normed, inverse, windows, probs))


def block_backward(grad_out, saved, gain, w_in, w_proj, offsets):
    normed, inverse, windows, probs = saved
    time_count, levels, lat_rows, lon_cols, features = grad_out.shape
    scale = HD ** (-0.5)
    flat = grad_out.reshape(-1, features)
    grad_ctx = lax.dot_general(
        flat, w_proj, (((1,), (1,)), ((), ())), preferred_element_type=jnp.float32
    ).astype(jnp.bfloat16)
    grad_win = to_windows(grad_ctx.reshape(time_count, levels, lat_rows, lon_cols, H * HD))
    count, span = (grad_win.shape[0], grad_win.shape[1])
    grad_win = grad_win.reshape(count, span, H, HD)
    parts = windows.reshape(count, span, 3, H, HD)
    query, keys, values = (parts[:, :, 0], parts[:, :, 1], parts[:, :, 2])
    weights = probs.astype(jnp.float32)
    grad_probs = jnp.einsum("nihd,njhd->nhij", grad_win, values, preferred_element_type=jnp.float32)
    grad_scores = weights * (grad_probs - jnp.sum(grad_probs * weights, -1, keepdims=True))
    bias_term = fold_table(jnp.sum(grad_scores, 0), offsets)
    scores_bf = grad_scores.astype(jnp.bfloat16)
    grad_query = (
        jnp.einsum("nhij,njhd->nihd", scores_bf, keys, preferred_element_type=jnp.float32) * scale
    ).astype(jnp.bfloat16)
    grad_keys = (
        jnp.einsum("nhij,nihd->njhd", scores_bf, query, preferred_element_type=jnp.float32) * scale
    ).astype(jnp.bfloat16)
    grad_values = jnp.einsum(
        "nhij,nihd->njhd", probs, grad_win, preferred_element_type=jnp.float32
    ).astype(jnp.bfloat16)
    grad_mixed = jnp.stack([grad_query, grad_keys, grad_values], 2).reshape(count, span, 3 * H * HD)
    grad_grid = from_windows(grad_mixed, time_count, lat_rows, lon_cols).reshape(-1, 3 * H * HD)
    grad_norm = lax.dot_general(
        grad_grid, w_in, (((1,), (1,)), ((), ())), preferred_element_type=jnp.float32
    )
    flat_normed = normed.reshape(-1, features)
    flat_inverse = inverse.reshape(-1, 1)
    gain_term = jnp.sum(grad_norm * flat_normed, 0)
    scaled = grad_norm * gain
    grad_field = flat_inverse * (
        scaled
        - jnp.mean(scaled, -1, keepdims=True)
        - flat_normed * jnp.mean(scaled * flat_normed, -1, keepdims=True)
    )
    grad_in = (flat.astype(jnp.float32) + grad_field).astype(jnp.bfloat16).reshape(grad_out.shape)
    return (grad_in, gain_term, bias_term)


def rows_forward(field):
    arrived = passed_along(field[:, :, :SH], "lat", -1)
    return jnp.concatenate([field[:, :, SH:], arrived], 2)


def cols_forward(field):
    arrived = passed_along(field[:, :, :, :SW], "lon", -1)
    return jnp.concatenate([field[:, :, :, SW:], arrived], 3)


def rows_backward(field):
    arrived = passed_along(field[:, :, field.shape[2] - SH :], "lat", 1)
    return jnp.concatenate([arrived, field[:, :, : field.shape[2] - SH]], 2)


def cols_backward(field):
    arrived = passed_along(field[:, :, :, field.shape[3] - SW :], "lon", 1)
    return jnp.concatenate([arrived, field[:, :, :, : field.shape[3] - SW]], 3)


def roll_ahead(field):
    return cols_forward(rows_forward(field))


def roll_behind(field):
    return rows_backward(cols_backward(field))


def fetch_block(w_qkv, w_out, index):
    return (
        lax.all_gather(w_qkv[index], ("lat", "lon"), axis=0, tiled=True),
        lax.all_gather(w_out[index], ("lat", "lon"), axis=0, tiled=True),
    )


def on_device(tokens, cotangent, w_qkv, w_out, gains, tables):
    time_count, levels, lat_rows, lon_cols, features = tokens.shape
    offsets = offset_table()
    row_ids = lax.broadcasted_iota(jnp.int32, (levels, lat_rows, lon_cols), 1)
    polar = lax.axis_index("lat") == lax.axis_size("lat") - 1
    region = jnp.where(polar & (row_ids >= lat_rows - SH), 1, 0).astype(jnp.int32)
    valid_two = jnp.tile(region_pairs(region), (time_count, 1, 1))
    valid_one = jnp.ones(valid_two.shape, jnp.bool_)
    bias_one = expand_table(tables[0], offsets)
    bias_two = expand_table(tables[1], offsets)
    in_one, proj_one = fetch_block(w_qkv, w_out, 0)
    first, saved_one = block_forward(tokens, gains[0], in_one, proj_one, bias_one, valid_one)
    in_two, proj_two = fetch_block(w_qkv, w_out, 1)
    second, saved_two = block_forward(
        roll_ahead(first), gains[1], in_two, proj_two, bias_two, valid_two
    )
    outputs = roll_behind(second)
    grad_two, gain_two, table_two = block_backward(
        roll_ahead(cotangent), saved_two, gains[1], in_two, proj_two, offsets
    )
    grad_one, gain_one, table_one = block_backward(
        roll_behind(grad_two), saved_one, gains[0], in_one, proj_one, offsets
    )
    grad_gains, grad_tables = lax.psum(
        (jnp.stack([gain_one, gain_two]), jnp.stack([table_one, table_two])), ("dp", "lat", "lon")
    )
    total = (
        time_count
        * lax.axis_size("dp")
        * levels
        * lat_rows
        * lax.axis_size("lat")
        * lon_cols
        * lax.axis_size("lon")
    )
    norm_scale = 1.0 / math.sqrt(total)
    return (outputs, grad_one, grad_gains * norm_scale, grad_tables * norm_scale)


def solution(mesh):
    return jax.shard_map(
        on_device,
        mesh=mesh,
        in_specs=(
            P("dp", None, "lat", "lon", None),
            P("dp", None, "lat", "lon", None),
            P(None, ("lat", "lon"), None),
            P(None, ("lat", "lon"), None),
            P(),
            P(),
        ),
        out_specs=(P("dp", None, "lat", "lon", None), P("dp", None, "lat", "lon", None), P(), P()),
        check_vma=False,
    )
```

profile of v0, /device:TPU:0, one launch (start us, length us, event | category | flops | bytes accessed | tf_op | source)
XLA Modules:
  0.0 1032.8 jit_solution(4460932138251609008)
XLA Ops:
  7.2 2.1 fusion.63
  15.3 1.3 fusion.18
  16.8 86.3 %gather_fusion = f32[46656,8]{1,0:T(8,128)} fusion(f32[8,1265]{0,1:T(8,128)S(1)} %bitcast.170, s32[47104]{0:T(1024)S(1)} %pad_clamp_fusion), kind=kCustom, calls=%fused_computation | custom fusion | bytes 3172608 | tf_op jit(solution)/shard_map/gather | solution.py:66
  103.2 14.7 %copy.61 = f32[8,216,216]{1,2,0:T(8,128)} copy(f32[8,216,216]{0,2,1:T(8,128)} %bitcast.172) | data formatting | bytes 2985984 | tf_op jit(solution)/shard_map/broadcast_in_dim;reshape | solution.py:98
  119.1 5.0 collective-permute-start.5
  124.1 2.7 fusion.10
  126.8 1.2 copy.58
  128.0 2.4 fusion.71
  131.0 0.9 copy-done
  132.0 1.2 fusion.26
  133.8 1.8 fusion.20
  137.4 86.3 %gather_fusion.1 = f32[46656,8]{1,0:T(8,128)} fusion(f32[8,1265]{0,1:T(8,128)S(1)} %bitcast.169, s32[47104]{0:T(1024)S(1)} %copy-done.14), kind=kCustom, calls=%fused_computation.1 | custom fusion | bytes 3172608 | tf_op jit(solution)/shard_map/gather | solution.py:66
  223.8 13.4 %copy.67 = f32[8,216,216]{1,2,0:T(8,128)S(1)} copy(f32[8,216,216]{0,2,1:T(8,128)} %bitcast.171) | data formatting | bytes 2985984 | tf_op jit(solution)/shard_map/broadcast_in_dim;reshape | solution.py:98
  237.2 2.1 pad_maximum_fusion.4
  239.3 1.9 reshape.548
  241.2 2.1 fusion.56
  243.8 2.6 convolution_convert_fusion.5
  246.3 1.8 copy.70
  248.1 4.9 collective-permute-done.1
  253.0 2.3 maximum_convert_fusion
  255.3 2.3 reshape.558
  257.6 1.3 fusion.62
  259.6 1.4 div.49
  260.9 1.4 multiply_reduce_fusion
  263.0 1.3 rsqrt.32
  264.3 4.0 fusion.13
  268.3 2.2 copy.64
  270.5 3.7 fusion.72
  274.2 2.2 fusion.16
  276.4 1.0 fusion.27
  277.4 1.1 fusion.28
  278.7 1.1 fusion.32
  279.8 1.0 fusion.33
  280.8 1.9 copy.69
  282.8 2.0 dot_general.72
  284.8 1.3 pad_maximum_fusion
  286.1 4.3 multiply_reduce_fusion.1
  290.4 1.1 add_convert_fusion.2
  291.6 1.9 reshape.550
  293.5 1.4 fusion.64
  295.0 2.0 fusion.39
  297.9 8.8 collective-permute-done.6
  308.2 2.3 reshape.553
  310.5 1.8 copy.80
  312.3 2.1 reshape.588
  314.4 12.6 %copy.81 = f32[46656,8]{1,0:T(8,128)} copy(f32[46656,8]{0,1:T(8,128)S(1)} %bitcast.178) | data formatting | bytes 2985984 | tf_op jit(solution)/shard_map/reshape | solution.py:70
  327.0 251.2 %scatter_custom_fusion.1 = f32[8,1265]{0,1:T(8,128)S(1)} fusion(s32[46656]{0:T(1024)} %copy-done.19, f32[46656,8]{1,0:T(8,128)} %copy.81, f32[]{:T(128)} %constant.18.clone.1), kind=kCustom, calls=%fused_computation.101 | custom fusion | flops 373248 | bytes 40992 | tf_op jit(solution)/shard_map/scatter-add | solution.py:74
  579.0 1.8 fusion.55
  581.3 1.9 fusion.40
  583.2 1.2 reshape.551
  584.5 2.6 convolution_convert_fusion.4
  587.1 1.1 copy.74
  588.1 1.1 fusion.29
  589.3 1.4 fusion.17
  591.9 1.1 fusion.30
  593.0 1.0 fusion.31
  594.8 1.3 pad_maximum_fusion.1
  596.1 4.3 multiply_reduce_fusion.2
  601.0 38.2 %psum.14 = f32[2,1024]{1,0:T(2,128)S(1)} all-reduce(f32[2,1024]{1,0:T(2,128)S(1)} %pad_maximum_fusion.8), channel_id=1, replica_groups=mesh['dp'=4,'lat'=2,'lon'=4] {'dp','lat','lon'}, use_global_device_ids=true, to_apply=%region_16.17 | all-reduce | flops 2048 | bytes 16384 | tf_op jit(solution)/shard_map/psum | solution.py:217
  640.0 12.6 %copy.79 = f32[46656,8]{1,0:T(8,128)} copy(f32[46656,8]{0,1:T(8,128)S(1)} %bitcast.179) | data formatting | bytes 2985984 | tf_op jit(solution)/shard_map/reshape | solution.py:70
  652.5 251.2 %scatter_custom_fusion = f32[8,1265]{0,1:T(8,128)S(1)} fusion(s32[46656]{0:T(1024)} %copy-done.19, f32[46656,8]{1,0:T(8,128)} %copy.79, f32[]{:T(128)} %constant.18.clone.1), kind=kCustom, calls=%fused_computation.103 | custom fusion | flops 373248 | bytes 40992 | tf_op jit(solution)/shard_map/scatter-add | solution.py:74
  905.6 2.0 fusion.41
  908.5 116.2 %all-reduce.2.cloned.1.call-done = f32[2,8,1265]{2,1,0:T(8,128)} async-done(((f32[2,8,1265]{2,1,0:T(8,128)}), f32[2,8,1265]{2,1,0:T(8,128)}) %all-reduce.2.cloned.1.call-update) | async-done | bytes 80976 | tf_op jit(solution)/shard_map/psum | solution.py:217
  1024.8 1.5 broadcast_multiply_fusion
  (144 shorter events, 22.0 us)
Async XLA Ops:
  7.2 2.3 copy-start.21
  7.2 3.8 copy-start.20
  7.2 116.9 %all-gather.9.cloned.1.call-start = ((), (), s32[]{:S(2)}) async-start(), calls=%async_computation.1 | async-start | bytes 3538944 | tf_op jit(solution)/shard_map/all_gather | solution.py:189
  9.4 2.6 copy-start.2
  9.4 124.4 %all-gather.11.cloned.1.call-start = ((), (), s32[]{:S(2)}) async-start(), calls=%async_computation.2 | async-start | bytes 1179648 | tf_op jit(solution)/shard_map/all_gather | solution.py:190
  10.2 233.6 %all-gather.15.cloned.1.call-start = ((), (), s32[]{:S(2)}) async-start(), calls=%async_computation.4 | async-start | bytes 1179648 | tf_op jit(solution)/shard_map/all_gather | solution.py:190
  10.9 253.4 %all-gather.13.cloned.1.call-start = ((), (), s32[]{:S(2)}) async-start(), calls=%async_computation.3 | async-start | bytes 3538944 | tf_op jit(solution)/shard_map/all_gather | solution.py:189
  11.0 107.1 %collective-permute-start.4 = (bf16[1,3,3,12,1024]{4,3,2,1,0:T(8,128)(2,1)S(1)}, bf16[1,3,3,12,1024]{4,3,2,1,0:T(8,128)(2,1)S(1)}, u32[]{:S(2)}, u32[]{:S(2)}) collective-permute-start(bf16[1,3,3,12,1024]{4,3,2,1,0:T(8,128)(2,1)S(1)} %get-tuple-element.35), channel_id=1, source_target_pairs={{0,4},{4,0},{1,5},{5,1},{2,6},{6,2},{3,7},{7,3},{8,12},{12,8},{9,1... | collective-permute-start | bytes 663560 | tf_op jit(solution)/shard_map/ppermute | solution.py:22
  11.6 2.4 copy-start.28
  11.6 3.1 copy-start.24
  11.6 1013.2 %all-reduce.2.cloned.1.call-start = ((), (), s32[]{:S(2)}) async-start(), calls=%async_computation | async-start | bytes 163840 | tf_op jit(solution)/shard_map/psum | solution.py:217
  14.0 1.3 copy-start.19
  15.3 87.9 %copy-start.13 = (s32[47104]{0:T(1024)}, s32[47104]{0:T(1024)S(1)}, u32[]{:S(2)}) copy-start(s32[47104]{0:T(1024)S(1)} %pad_clamp_fusion) | copy-start | bytes 565252
  119.1 118.1 %collective-permute-start.5 = (bf16[1,3,6,6,1024]{4,3,2,1,0:T(8,128)(2,1)}, bf16[1,3,6,6,1024]{4,3,2,1,0:T(8,128)(2,1)}, u32[]{:S(2)}, u32[]{:S(2)}) collective-permute-start(bf16[1,3,6,6,1024]{4,3,2,1,0:T(8,128)(2,1)} %get-tuple-element.33), channel_id=1, source_target_pairs={{0,3},{1,0},{2,1},{3,2},{4,7},{5,4},{6,5},{7,6},{8,11},{9,8},{10,9... | collective-permute-start | bytes 663560 | tf_op jit(solution)/shard_map/ppermute | solution.py:22
  130.4 0.6 copy-start.25
  131.0 0.9 copy-start
  133.8 3.4 copy-start.22
  133.8 3.7 copy-start.14
  136.5 104.7 %collective-permute-start = (bf16[1,3,3,12,1024]{4,3,2,1,0:T(8,128)(2,1)}, bf16[1,3,3,12,1024]{4,3,2,1,0:T(8,128)(2,1)}, u32[]{:S(2)}, u32[]{:S(2)}) collective-permute-start(bf16[1,3,3,12,1024]{4,3,2,1,0:T(8,128)(2,1)} %get-tuple-element.31), channel_id=1, source_target_pairs={{0,4},{4,0},{1,5},{5,1},{2,6},{6,2},{3,7},{7,3},{8,12},{12,8},{9,1... | collective-permute-start | bytes 663560 | tf_op jit(solution)/shard_map/ppermute | solution.py:22
  243.3 9.7 collective-permute-start.1
  274.2 2.2 copy-start.4
  274.2 3.2 copy-start.17
  286.1 4.3 copy-start.5
  286.1 4.3 copy-start.9
  286.1 4.3 copy-start.27
  286.1 4.3 copy-start.31
  286.1 4.3 copy-start.32
  294.9 11.8 %copy-start.11 = (bf16[1,3,6,6,1024]{4,3,2,1,0:T(8,128)(2,1)}, bf16[1,3,6,6,1024]{4,3,2,1,0:T(8,128)(2,1)S(1)}, u32[]{:S(2)}) copy-start(bf16[1,3,6,6,1024]{4,3,2,1,0:T(8,128)(2,1)S(1)} %get-tuple-element.25) | copy-start | bytes 663556
  294.9 11.8 %collective-permute-start.6 = (bf16[1,3,6,6,1024]{4,3,2,1,0:T(8,128)(2,1)S(1)}, bf16[1,3,6,6,1024]{4,3,2,1,0:T(8,128)(2,1)S(1)}, u32[]{:S(2)}, u32[]{:S(2)}) collective-permute-start(bf16[1,3,6,6,1024]{4,3,2,1,0:T(8,128)(2,1)S(1)} %get-tuple-element.24), channel_id=1, source_target_pairs={{0,1},{1,2},{2,3},{3,0},{4,5},{5,6},{6,7},{7,4},{8,9},{9,10},{10,1... | collective-permute-start | bytes 663560 | tf_op jit(solution)/shard_map/ppermute | solution.py:22
  297.9 281.1 %collective-permute-start.2 = (bf16[1,3,6,6,1024]{4,3,2,1,0:T(8,128)(2,1)}, bf16[1,3,6,6,1024]{4,3,2,1,0:T(8,128)(2,1)}, u32[]{:S(2)}, u32[]{:S(2)}) collective-permute-start(bf16[1,3,6,6,1024]{4,3,2,1,0:T(8,128)(2,1)} %get-tuple-element.26), channel_id=1, source_target_pairs={{0,1},{1,2},{2,3},{3,0},{4,5},{5,6},{6,7},{7,4},{8,9},{9,10},{10,1... | collective-permute-start | bytes 663560 | tf_op jit(solution)/shard_map/ppermute | solution.py:22
  306.7 0.9 copy-start.15
  307.5 273.8 %collective-permute-start.7 = (bf16[1,3,3,12,1024]{4,3,2,1,0:T(8,128)(2,1)}, bf16[1,3,3,12,1024]{4,3,2,1,0:T(8,128)(2,1)}, u32[]{:S(2)}, u32[]{:S(2)}) collective-permute-start(bf16[1,3,3,12,1024]{4,3,2,1,0:T(8,128)(2,1)} %fusion.53), channel_id=1, source_target_pairs={{0,4},{4,0},{1,5},{5,1},{2,6},{6,2},{3,7},{7,3},{8,12},{12,8},{9,1... | collective-permute-start | bytes 663560 | tf_op jit(solution)/shard_map/ppermute | solution.py:22
  327.0 254.3 %copy-start.12 = (bf16[1,3,6,6,1024]{4,3,2,1,0:T(8,128)(2,1)S(1)}, bf16[1,3,6,6,1024]{4,3,2,1,0:T(8,128)(2,1)}, u32[]{:S(2)}) copy-start(bf16[1,3,6,6,1024]{4,3,2,1,0:T(8,128)(2,1)} %copy-done.11) | copy-start | bytes 663556
  327.0 254.3 %copy-start.16 = (bf16[1,3,6,6,1024]{4,3,2,1,0:T(8,128)(2,1)S(1)}, bf16[1,3,6,6,1024]{4,3,2,1,0:T(8,128)(2,1)}, u32[]{:S(2)}) copy-start(bf16[1,3,6,6,1024]{4,3,2,1,0:T(8,128)(2,1)} %copy-done.15) | copy-start | bytes 663556
  580.8 324.9 %collective-permute-start.3 = (bf16[1,3,3,12,1024]{4,3,2,1,0:T(8,128)(2,1)}, bf16[1,3,3,12,1024]{4,3,2,1,0:T(8,128)(2,1)}, u32[]{:S(2)}, u32[]{:S(2)}) collective-permute-start(bf16[1,3,3,12,1024]{4,3,2,1,0:T(8,128)(2,1)} %fusion.55), channel_id=1, source_target_pairs={{0,4},{4,0},{1,5},{5,1},{2,6},{6,2},{3,7},{7,3},{8,12},{12,8},{9,1... | collective-permute-start | bytes 663560 | tf_op jit(solution)/shard_map/ppermute | solution.py:22
  583.2 4.9 copy-start.1
  584.5 4.8 copy-start.6
  589.3 1.4 copy-start.26
  590.7 1.1 copy-start.3
  596.1 4.9 copy-start.33
  639.9 264.1 %copy-start.23 = (f32[1,8,1265]{2,1,0:T(8,128)S(1)}, f32[1,8,1265]{2,1,0:T(8,128)}, u32[]{:S(2)}) copy-start(f32[1,8,1265]{2,1,0:T(8,128)} %copy.83) | copy-start | bytes 121444
  639.9 264.7 %copy-start.18 = (f32[216,1024]{1,0:T(8,128)S(1)}, f32[216,1024]{1,0:T(8,128)}, u32[]{:S(2)}) copy-start(f32[216,1024]{1,0:T(8,128)} %get-tuple-element.52) | copy-start | bytes 2654212
  640.0 264.7 %copy-start.29 = (f32[216]{0:T(256)S(1)}, f32[216]{0:T(256)}, u32[]{:S(2)}) copy-start(f32[216]{0:T(256)} %broadcast_multiply_fusion.5) | copy-start | bytes 2596
  640.0 264.7 %copy-start.30 = (f32[216]{0:T(256)S(1)}, f32[216]{0:T(256)}, u32[]{:S(2)}) copy-start(f32[216]{0:T(256)} %rsqrt.33) | copy-start | bytes 2596
  652.5 252.2 %copy-start.7 = (bf16[216,1024]{1,0:T(8,128)(2,1)S(1)}, bf16[216,1024]{1,0:T(8,128)(2,1)}, u32[]{:S(2)}) copy-start(bf16[216,1024]{1,0:T(8,128)(2,1)} %copy-done.6) | copy-start | bytes 1327108
  652.5 252.2 %copy-start.8 = (f32[216,1024]{1,0:T(8,128)S(1)}, f32[216,1024]{1,0:T(8,128)}, u32[]{:S(2)}) copy-start(f32[216,1024]{1,0:T(8,128)} %reshape.553) | copy-start | bytes 2654212
  903.8 1.8 copy-start.10
Sparse Core Ops, SparseCore 0:
  10.2 40.9 all-gather.8
  52.8 20.9 all-gather.10
  75.4 21.7 all-gather.14
  98.6 42.1 all-gather.12
  904.8 119.9 all-reduce.1
where the time goes:
time: 1040 us; the launch traced here: 1030 us
  other arithmetic  532 us (51%)
  local copies, waits for them, and re-layouts  268 us (26%)
  waiting for transfers between devices  131 us (13%)
  matrix products  42.5 us (4%)
  blocking collectives  38.2 us (4%)
  between operations  14.4 us (1%)
    scatter-add x2, other arithmetic, fold_table(): return jnp.zeros((H, (2 * Z - 1) * (2 * WH - 1) * (2 * WW - 1)), jnp.floa...  502 us
    gather x2, local copies, waits for them, and re-layouts, expand_table(): return table[:, offsets].reshape(H, span, span)  173 us
    psum x1, waiting for transfers between devices, on_device(): lax.psum((jnp.stack([gain_one, gain_two]), jnp.stack([table_one, table_tw...  116 us
    psum x1, blocking collectives, on_device(): lax.psum((jnp.stack([gain_one, gain_two]), jnp.stack([table_one, table_tw...  38.2 us
    another operation x2, local copies, waits for them, and re-layouts, block_forward(): bias[None]  28.1 us
    reshape x4, local copies, waits for them, and re-layouts, fold_table(): summed = full.reshape(H, -1)  28 us
  transfers between devices with their start and end apart: 13, of which 3 were waited for; matrix products, arithmetic and copies ran while one was open for 78% of the time, Pallas kernels for 0%

commit v1 on v0

v1 whole, which is shorter than its diff:
```python
import functools
import math

import jax
import jax.numpy as jnp
import numpy as np
from jax import lax
from jax.experimental import pallas as pl
from jax.experimental.pallas import tpu as pltpu
from jax.sharding import PartitionSpec as P

MESH = pl.DeviceIdType.MESH
HD = 64
H = 8
Z = 3
WH = 6
WW = 12
SH = 3
SW = 6
EPS = 1e-05
RELS = (2 * Z - 1) * (2 * WH - 1) * (2 * WW - 1)
STEP_Z = (2 * WH - 1) * (2 * WW - 1)
STEP_Y = 2 * WW - 1
CENTRE = (Z - 1) * STEP_Z + (WH - 1) * STEP_Y + WW - 1
QR = 64
ROWS = 4 * QR
SPAN = 640
TABLE = 1280
GROUPS = Z * SH
LINES = Z * WH
LINE = 16
SCALE = HD ** (-0.5)
FAR = -1e30
VMEM_LIMIT = 58 * 1024 * 1024


def token_places():
    places = []
    for row in range(ROWS):
        quad, inner = divmod(row, QR)
        if inner >= GROUPS * SW:
            places.append(None)
            continue
        group, x = divmod(inner, SW)
        z, y = divmod(group, SH)
        places.append((z, y + SH * (quad // 2), x + SW * (quad % 2)))
    return places


def order_matrix():
    order = np.zeros((ROWS, LINES * LINE), np.float32)
    for row, place in enumerate(token_places()):
        if place is not None:
            z, y, x = place
            order[row, (z * WH + y) * LINE + x] = 1
    return order


def spread_matrix():
    spread = np.zeros((SPAN, ROWS), np.float32)
    for row, place in enumerate(token_places()):
        if place is not None:
            z, y, x = place
            spread[z * STEP_Z + y * STEP_Y + x, row] = 1
    return spread


def group_list():
    groups = []
    for quad in range(4):
        for group in range(GROUPS):
            z, y = divmod(group, SH)
            start = z * STEP_Z + (y + SH * (quad // 2)) * STEP_Y + SW * (quad % 2)
            groups.append((quad * QR + group * SW, CENTRE - start))
    return groups


def dot(a, b):
    return jnp.dot(a, b, preferred_element_type=jnp.float32)


def dot_t(a, b):
    return lax.dot_general(a, b, (((1,), (1,)), ((), ())), preferred_element_type=jnp.float32)


def t_dot(a, b):
    return lax.dot_general(a, b, (((0,), (0,)), ((), ())), preferred_element_type=jnp.float32)


def prep_kernel(tok, cot, tab, order, spread, flag, x_out, g_out, bias_out, lines, rows):
    lines[...] = jnp.zeros_like(lines)
    for source, target in ((tok, x_out), (cot, g_out)):
        for k in range(LINES):
            lines[k, 0:WW, :] = source[k // WH, k % WH]
        flat = lines[...].reshape(LINES * LINE, lines.shape[2])
        target[...] = dot(order[...], flat).astype(jnp.bfloat16)
    rows[...] = jnp.zeros_like(rows)
    key = lax.broadcasted_iota(jnp.int32, (ROWS, ROWS), 1)
    query = lax.broadcasted_iota(jnp.int32, (ROWS, ROWS), 0)
    pad = key % QR >= GROUPS * SW
    apart = (key // (2 * QR)) != (query // (2 * QR))
    drop_two = pad | (apart & (flag[0] == 1))

    def one_head(n, carry):
        base = jnp.broadcast_to(tab[n], (8, TABLE))
        base = pltpu.roll(base, 0, 1, stride=1, stride_axis=0)
        for row, shift in group_list():
            rows[row : row + SW, :] = pltpu.roll(base, TABLE - shift, 1)[:SW, :SPAN]
        wide = rows[...]
        high = wide.astype(jnp.bfloat16)
        rest = wide - high.astype(jnp.float32)
        mid = rest.astype(jnp.bfloat16)
        low = (rest - mid.astype(jnp.float32)).astype(jnp.bfloat16)
        part = spread[...]
        bias = dot(high, part) + dot(mid, part) + dot(low, part)
        bias_out[n] = bias
        return carry

    lax.fori_loop(0, 2 * H, one_head, 0)

    def mask_head(n, carry):
        bias_out[n] = jnp.where(pad, FAR, bias_out[n])
        bias_out[n + H] = jnp.where(drop_two, FAR, bias_out[n + H])
        return carry

    lax.fori_loop(0, H, mask_head, 0)


def normalise(values):
    centred = values - jnp.mean(values, -1, keepdims=True)
    inverse = lax.rsqrt(jnp.mean(centred * centred, -1, keepdims=True) + EPS)
    return centred * inverse, inverse


def half_mask(which):
    lane = lax.broadcasted_iota(jnp.int32, (ROWS, 2 * HD), 1)
    return (lane // HD) == which


def forward_kernel(x_ref, gain, w_in, w_proj, bias, y_out, qkv, probs, ctx):
    normed, _ = normalise(x_ref[...].astype(jnp.float32))
    qkv[...] = dot((normed * gain[...]).astype(jnp.bfloat16), w_in[...]).astype(jnp.bfloat16)
    first_half = half_mask(0)
    for pair in range(H // 2):
        lo, hi = pair * 2 * HD, (pair + 1) * 2 * HD
        query = qkv[:, lo:hi] * jnp.bfloat16(SCALE)
        keys = qkv[:, H * HD + lo : H * HD + hi]
        values = qkv[:, 2 * H * HD + lo : 2 * H * HD + hi]
        found = []
        for side in range(2):
            keep = first_half if side == 0 else ~first_half
            scores = dot_t(jnp.where(keep, query, 0), keys) + bias[2 * pair + side]
            powers = jnp.exp(scores - jnp.max(scores, -1, keepdims=True))
            weights = (powers / jnp.sum(powers, -1, keepdims=True)).astype(jnp.bfloat16)
            probs[2 * pair + side] = weights
            found.append(dot(weights, values))
        ctx[:, lo:hi] = jnp.where(first_half, found[0], found[1]).astype(jnp.bfloat16)
    y_out[...] = (x_ref[...].astype(jnp.float32) + dot(ctx[...], w_proj[...])).astype(jnp.bfloat16)


def backward_core(g_ref, x_ref, gain, w_in, w_proj, qkv, probs, collect, gain_out, table_out,
                  gctx, gqkv, wide):
    gctx[...] = dot_t(g_ref[...], w_proj[...]).astype(jnp.bfloat16)
    first_half = half_mask(0)
    row_in_group = lax.broadcasted_iota(jnp.int32, (8, SPAN), 0) < SW
    zeros = jnp.zeros((8, TABLE - SPAN), jnp.float32)
    for pair in range(H // 2):
        lo, hi = pair * 2 * HD, (pair + 1) * 2 * HD
        query = qkv[:, lo:hi]
        keys = qkv[:, H * HD + lo : H * HD + hi]
        values = qkv[:, 2 * H * HD + lo : 2 * H * HD + hi]
        part = gctx[:, lo:hi]
        grads = []
        for side in range(2):
            head = 2 * pair + side
            keep = first_half if side == 0 else ~first_half
            weights_bf = probs[head]
            weights = weights_bf.astype(jnp.float32)
            grad_probs = dot_t(jnp.where(keep, part, 0), values)
            grad_scores = weights * (
                grad_probs - jnp.sum(grad_probs * weights, -1, keepdims=True)
            )
            s = grad_scores.astype(jnp.bfloat16)
            rest = (grad_scores - s.astype(jnp.float32)).astype(jnp.bfloat16)
            wide[head] = dot(s, collect[...]) + dot(rest, collect[...])
            grads.append((dot(s, keys), t_dot(s, query), t_dot(weights_bf, part)))
        for which, factor in ((0, SCALE), (1, SCALE), (2, 1.0)):
            both = jnp.where(first_half, grads[0][which], grads[1][which]) * factor
            at = which * H * HD
            gqkv[:, at + lo : at + hi] = both.astype(jnp.bfloat16)

    def fold(head, carry):
        total = jnp.zeros((8, TABLE), jnp.float32)
        for row, shift in group_list():
            rows = jnp.where(row_in_group, wide[head, row : row + 8, :], 0.0)
            total = total + pltpu.roll(jnp.concatenate([rows, zeros], 1), shift, 1)
        line = total[0:1]
        for x in range(1, SW):
            line = line + pltpu.roll(total[x : x + 1], TABLE - x, 1)
        table_out[head] = line
        return carry

    lax.fori_loop(0, H, fold, 0)
    grad_u = dot_t(gqkv[...], w_in[...])
    normed, inverse = normalise(x_ref[...].astype(jnp.float32))
    gain_out[...] = jnp.sum(grad_u * normed, 0, keepdims=True)
    scaled = grad_u * gain[...]
    return g_ref[...].astype(jnp.float32) + inverse * (
        scaled
        - jnp.mean(scaled, -1, keepdims=True)
        - normed * jnp.mean(scaled * normed, -1, keepdims=True)
    )


def backward_kernel(g_ref, x_ref, gain, w_in, w_proj, qkv, probs, collect,
                    gx_out, gain_out, table_out, gctx, gqkv, wide):
    grad = backward_core(g_ref, x_ref, gain, w_in, w_proj, qkv, probs, collect, gain_out,
                         table_out, gctx, gqkv, wide)
    gx_out[...] = grad.astype(jnp.bfloat16)


def last_kernel(g_ref, x_ref, gain, w_in, w_proj, qkv, probs, collect, y_ref, order,
                gx_out, gain_out, table_out, y_out, gctx, gqkv, wide):
    grad = backward_core(g_ref, x_ref, gain, w_in, w_proj, qkv, probs, collect, gain_out,
                         table_out, gctx, gqkv, wide)
    for source, target in ((grad.astype(jnp.bfloat16), gx_out), (y_ref[...], y_out)):
        lines = t_dot(order[...], source).astype(jnp.bfloat16)
        for k in range(LINES):
            target[k // WH, k % WH] = lines[k * LINE : k * LINE + WW]


def exchange_kernel(ahead, src, dst, send, recv, own):
    lat, lon = lax.axis_index("lat"), lax.axis_index("lon")
    lats, lons = lax.axis_size("lat"), lax.axis_size("lon")

    def to(quad, sign):
        y, x = quad // 2, quad % 2
        if ahead:
            dy, dx = 1 - y, 1 - x
        else:
            dy, dx = y, x
        return {
            "lat": lax.rem(lat + lats + sign * dy, lats),
            "lon": lax.rem(lon + lons + sign * dx, lons),
        }

    sign = -1 if ahead else 1
    moving = [quad for quad in range(4) if quad != (3 if ahead else 0)]
    barrier = pltpu.get_barrier_semaphore()
    for quad in moving:
        pl.semaphore_signal(barrier, inc=1, device_id=to(quad, -sign), device_id_type=MESH)
    stay = 3 if ahead else 0
    local = pltpu.make_async_copy(src.at[stay], dst.at[3 - stay], own)
    local.start()
    pl.semaphore_wait(barrier, 3)
    copies = []
    for n, quad in enumerate(moving):
        copies.append(
            pltpu.make_async_remote_copy(
                src_ref=src.at[quad],
                dst_ref=dst.at[3 - quad],
                send_sem=send.at[n],
                recv_sem=recv.at[n],
                device_id=to(quad, sign),
                device_id_type=MESH,
            )
        )
        copies[-1].start()
    local.wait()
    for copy in copies:
        copy.wait()


def exchange(field, ahead, number):
    quads = field.reshape(4, QR, field.shape[-1])
    moved = pl.pallas_call(
        functools.partial(exchange_kernel, ahead),
        out_shape=jax.ShapeDtypeStruct(quads.shape, quads.dtype),
        in_specs=[pl.BlockSpec(memory_space=pltpu.VMEM)],
        out_specs=pl.BlockSpec(memory_space=pltpu.VMEM),
        scratch_shapes=[
            pltpu.SemaphoreType.DMA((3,)),
            pltpu.SemaphoreType.DMA((3,)),
            pltpu.SemaphoreType.DMA,
        ],
        compiler_params=pltpu.CompilerParams(collective_id=number, has_side_effects=True),
    )(quads)
    return moved.reshape(field.shape)


def call(kernel, out, scratch, args, smem=(), flops=10**9):
    specs = [
        pl.BlockSpec(memory_space=pltpu.SMEM if n in smem else pltpu.VMEM)
        for n in range(len(args))
    ]
    return pl.pallas_call(
        kernel,
        out_shape=[jax.ShapeDtypeStruct(shape, dtype) for shape, dtype in out],
        in_specs=specs,
        out_specs=[pl.BlockSpec(memory_space=pltpu.VMEM) for _ in out],
        scratch_shapes=[pltpu.VMEM(shape, dtype) for shape, dtype in scratch],
        compiler_params=pltpu.CompilerParams(vmem_limit_bytes=VMEM_LIMIT),
        cost_estimate=pl.CostEstimate(flops=flops, bytes_accessed=8 * 2**20, transcendentals=0),
    )(*args)


def fetch_block(w_qkv, w_out, index):
    return (
        lax.all_gather(w_qkv[index], ("lat", "lon"), axis=0, tiled=True),
        lax.all_gather(w_out[index], ("lat", "lon"), axis=0, tiled=True),
    )


def on_device(tokens, cotangent, w_qkv, w_out, gains, tables):
    features = tokens.shape[-1]
    bf, f32 = jnp.bfloat16, jnp.float32
    inner = H * HD
    order = jnp.asarray(order_matrix(), bf)
    spread = jnp.asarray(spread_matrix(), bf)
    collect = jnp.asarray(spread_matrix().T.copy(), bf)
    in_one, proj_one = fetch_block(w_qkv, w_out, 0)
    in_two, proj_two = fetch_block(w_qkv, w_out, 1)
    polar = lax.axis_index("lat") == lax.axis_size("lat") - 1
    flag = jnp.where(polar, 1, 0).astype(jnp.int32).reshape(1)
    lines = jnp.pad(tables.reshape(2 * H, 1, RELS)[:, :, ::-1], ((0, 0), (0, 0), (0, TABLE - RELS)))
    field = ((ROWS, features), bf)
    x_one, g_out, bias = call(
        prep_kernel,
        [field, field, ((2 * H, ROWS, ROWS), f32)],
        [((LINES, LINE, features), bf), ((ROWS, SPAN), f32)],
        (tokens[0], cotangent[0], lines, order, spread, flag),
        smem=(5,),
        flops=8 * 10**9,
    )
    saved = [((ROWS, 3 * inner), bf), ((H, ROWS, ROWS), bf)]
    wide = [((ROWS, inner), bf)]
    g_two = exchange(g_out, True, 0)
    gain_one, gain_two = gains[0:1], gains[1:2]
    first, qkv_one, probs_one = call(
        forward_kernel, [field] + saved, wide, (x_one, gain_one, in_one, proj_one, bias[:H])
    )
    x_two = exchange(first, True, 1)
    second, qkv_two, probs_two = call(
        forward_kernel, [field] + saved, wide, (x_two, gain_two, in_two, proj_two, bias[H:])
    )
    y_back = exchange(second, False, 2)
    back = [((ROWS, inner), bf), ((ROWS, 3 * inner), bf), ((H, ROWS, SPAN), f32)]
    terms = [((1, features), f32), ((H, 1, TABLE), f32)]
    gx_two, gterm_two, tterm_two = call(
        backward_kernel,
        [field] + terms,
        back,
        (g_two, x_two, gain_two, in_two, proj_two, qkv_two, probs_two, collect),
    )
    g_one = exchange(gx_two, False, 3)
    window = (tokens.shape[1:], bf)
    grad_tokens, gterm_one, tterm_one, outputs = call(
        last_kernel,
        [window] + terms + [window],
        back,
        (g_one, x_one, gain_one, in_one, proj_one, qkv_one, probs_one, collect, y_back, order),
    )
    packed = jnp.concatenate(
        [gterm_one, gterm_two, tterm_one.reshape(1, -1), tterm_two.reshape(1, -1)], 1
    )
    packed = lax.psum(packed, ("dp", "lat", "lon"))
    total = math.prod(tokens.shape[:4]) * math.prod(
        lax.axis_size(axis) for axis in ("dp", "lat", "lon")
    )
    packed = packed * (1.0 / math.sqrt(total))
    grad_gains = packed[:, : 2 * features].reshape(2, features)
    folded = packed[:, 2 * features :].reshape(2, H, TABLE)
    grad_tables = folded[:, :, :RELS][:, :, ::-1]
    return (outputs[None], grad_tokens[None], grad_gains, grad_tables)


def solution(mesh):
    return jax.shard_map(
        on_device,
        mesh=mesh,
        in_specs=(
            P("dp", None, "lat", "lon", None),
            P("dp", None, "lat", "lon", None),
            P(None, ("lat", "lon"), None),
            P(None, ("lat", "lon"), None),
            P(),
            P(),
        ),
        out_specs=(P("dp", None, "lat", "lon", None), P("dp", None, "lat", "lon", None), P(), P()),
        check_vma=False,
    )
```

time: 1040 us -> 329 us (0.32)
  other arithmetic: 532 us -> 2.47 us
  local copies, waits for them, and re-layouts: 268 us -> 13.6 us
  Pallas kernels: 0 us -> 111 us
  waiting for transfers between devices: 131 us -> 187 us
  matrix products: 42.5 us -> 0 us
  blocking collectives: 38.2 us -> 0 us
    scatter-add x2 -> x0, other arithmetic: 502 us -> none  [fold_table(): return jnp.zeros((H, (2 * Z - 1) * (2 * WH - 1) * (2 * WW - 1)), jnp.floa...]
    gather x2 -> x0, local copies, waits for them, and re-layouts: 173 us -> none  [expand_table(): return table[:, offsets].reshape(H, span, span)]
    pallas_call x0 -> x9, Pallas kernels: none -> 111 us  [the longest x5 57.4 us: call(): pl.pallas_call(kernel, out_shape=[jax.ShapeDtypeStruct(shape, dtype) for...]
    all_gather x2, waiting for transfers between devices: 0.01 us -> 63.8 us  [fetch_block(): lax.all_gather(w_qkv[index], ('lat', 'lon'), axis=0, tiled=True)]
    psum x1 -> x0, blocking collectives: 38.2 us -> none  [on_device(): lax.psum((jnp.stack([gain_one, gain_two]), jnp.stack([table_one, table_tw...]
    dot_general x18 -> x0, matrix products: 36.4 us -> none  [the longest x2 8.51 us: block_backward(): lax.dot_general(grad_grid, w_in, (((1,), (1,)), ((), ())), preferred_elem...]
    reshape x10 -> x3, local copies, waits for them, and re-layouts: 36.4 us -> 0.71 us  [the longest x1 0.61 us: on_device(): grad_gains = packed[:, :2 * features].reshape(2, features)]
    another operation x5 -> x0, local copies, waits for them, and re-layouts: 29.4 us -> none  [the longest x2 28.1 us: block_forward(): bias[None]]
  transfers between devices with their start and end apart: 13 -> 5, of which waited for: 3 -> 4; matrix products, arithmetic and copies ran while one was open for 78% -> 3% of each run, Pallas kernels for 0% -> 16%
where the time goes in v1:
time: 329 us; the launch traced here: 328 us
  waiting for transfers between devices  187 us (57%)
  Pallas kernels  111 us (34%)
  between operations  13.9 us (4%)
  local copies, waits for them, and re-layouts  13.6 us (4%)
    psum x1, waiting for transfers between devices, on_device(): packed = lax.psum(packed, ('dp', 'lat', 'lon'))  118 us
    all_gather x2, waiting for transfers between devices, fetch_block(): lax.all_gather(w_qkv[index], ('lat', 'lon'), axis=0, tiled=True)  63.8 us
    pallas_call x5, Pallas kernels, call(): pl.pallas_call(kernel, out_shape=[jax.ShapeDtypeStruct(shape, dtype) for...  57.4 us
    pallas_call x4, Pallas kernels, exchange(): pl.pallas_call(functools.partial(exchange_kernel, ahead), out_shape=jax.S...  53.9 us
  transfers between devices with their start and end apart: 5, of which 4 were waited for; matrix products, arithmetic and copies ran while one was open for 3% of the time, Pallas kernels for 16%

profile of v1, /device:TPU:0, one launch (start us, length us, event | category | flops | bytes accessed | tf_op | source)
XLA Modules:
  0.0 328.0 jit_solution(12895103923613916894)
XLA Ops:
  7.2 0.0 copy-start
  7.2 0.0 all-gather.11.cloned.1.call-start
  7.2 1.7 fusion.2
  8.9 0.0 all-gather.11.cloned.1.call-update
  8.9 0.0 all-gather.9.cloned.1.call-start
  9.0 2.1 fusion.1
  11.0 0.0 all-gather.9.cloned.1.call-update
  11.1 0.0 all-gather.15.cloned.1.call-start
  11.1 0.7 all-gather.15.cloned.1.call-update
  11.8 0.0 all-gather.13.cloned.1.call-start
  11.9 0.5 all-gather.13.cloned.1.call-update
  12.4 0.0 all-reduce.3.cloned.1.call-start
  12.4 0.0 copy-done
  12.4 0.1 reshape.50
  12.5 1.2 reverse
  13.7 0.2 slice.49
  14.0 0.7 pad.4.tab
  14.7 0.0 copy-start.2
  14.7 16.9 %shard_map.120 = (bf16[256,1024]{1,0:T(8,128)(2,1)}, bf16[256,1024]{1,0:T(8,128)(2,1)}, f32[16,256,256]{2,1,0:T(8,128)}) custom-call(bf16[3,6,12,1024]{3,2,1,0:T(8,128)(2,1)} %bitcast.42, bf16[3,6,12,1024]{3,2,1,0:T(8,128)(2,1)} %bitcast.43, f32[16,1,1280]{2,1,0:T(1,128)} %pad.4.tab, bf16[256,288]{1,0:T(8,128)(2,1)} %constant.20.clone.order, ...), custom_call_target="tpu_custom_call" | custom-call | flops 8000000000 | bytes 8388608 | tf_op jit(solution)/shard_map/pallas_call | solution.py:296
  31.6 13.1 %shard_map.121 = bf16[4,64,1024]{2,1,0:T(8,128)(2,1)} custom-call(bf16[4,64,1024]{2,1,0:T(8,128)(2,1)} %bitcast.37), custom_call_target="tpu_custom_call" | custom-call | tf_op jit(solution)/shard_map/pallas_call | solution.py:276
  44.7 0.0 copy-done.2
  44.7 0.6 fusion.3
  45.3 4.7 %fusion = (f32[8,256,256]{2,1,0:T(8,128)}, f32[8,256,256]{2,1,0:T(8,128)}) fusion(f32[16,256,256]{2,1,0:T(8,128)} %get-tuple-element.22), kind=kLoop, calls=%fused_computation.4 | loop fusion | bytes 8388608 | tf_op jit(solution)/shard_map/slice | solution.py:344
  50.0 0.0 all-gather.11.cloned.1.call-done
  50.0 24.0 %all-gather.9.cloned.1.call-done = bf16[1,1024,1536]{2,1,0:T(8,128)(2,1)} async-done(((bf16[1,128,1536]{2,1,0:T(8,128)(2,1)}), bf16[1,1024,1536]{2,1,0:T(8,128)(2,1)}) %all-gather.9.cloned.1.call-update) | async-done | bytes 3145744 | tf_op jit(solution)/shard_map/all_gather | solution.py:309
  74.0 6.6 %shard_map.122 = (bf16[256,1024]{1,0:T(8,128)(2,1)}, bf16[256,1536]{1,0:T(8,128)(2,1)}, bf16[8,256,256]{2,1,0:T(8,128)(2,1)}) custom-call(bf16[256,1024]{1,0:T(8,128)(2,1)} %get-tuple-element.21.x_ref, f32[1,1024]{1,0:T(1,128)} %get-tuple-element.43.gain, bf16[1024,1536]{1,0:T(8,128)(2,1)} %bitcast.22, bf16[512,1024]{1,0:T(8,128)(2,1)} %bitcast.28, ...), custom_call_target="tpu_custom_call" | custom-call | flops 1000000000 | bytes 8388608 | tf_op jit(solution)/shard_map/pallas_call | solution.py:296
  80.6 17.1 %shard_map.123 = bf16[4,64,1024]{2,1,0:T(8,128)(2,1)} custom-call(bf16[4,64,1024]{2,1,0:T(8,128)(2,1)} %bitcast.38), custom_call_target="tpu_custom_call" | custom-call | tf_op jit(solution)/shard_map/pallas_call | solution.py:276
  97.7 3.2 all-gather.15.cloned.1.call-done
  100.9 39.8 %all-gather.13.cloned.1.call-done = bf16[1,1024,1536]{2,1,0:T(8,128)(2,1)} async-done(((bf16[1,128,1536]{2,1,0:T(8,128)(2,1)}), bf16[1,1024,1536]{2,1,0:T(8,128)(2,1)}) %all-gather.13.cloned.1.call-update) | async-done | bytes 3145744 | tf_op jit(solution)/shard_map/all_gather | solution.py:309
  140.7 6.7 %shard_map.124 = (bf16[256,1024]{1,0:T(8,128)(2,1)}, bf16[256,1536]{1,0:T(8,128)(2,1)}, bf16[8,256,256]{2,1,0:T(8,128)(2,1)}) custom-call(bf16[256,1024]{1,0:T(8,128)(2,1)} %bitcast.26, f32[1,1024]{1,0:T(1,128)} %get-tuple-element.42.gain, bf16[1024,1536]{1,0:T(8,128)(2,1)} %bitcast.24, bf16[512,1024]{1,0:T(8,128)(2,1)} %bitcast.30, ...), custom_call_target="tpu_custom_call" | custom-call | flops 1000000000 | bytes 8388608 | tf_op jit(solution)/shard_map/pallas_call | solution.py:296
  147.3 13.3 %shard_map.125 = (bf16[256,1024]{1,0:T(8,128)(2,1)}, f32[1,1024]{1,0:T(1,128)}, f32[8,1,1280]{2,1,0:T(1,128)}) custom-call(bf16[256,1024]{1,0:T(8,128)(2,1)} %bitcast.32, bf16[256,1024]{1,0:T(8,128)(2,1)} %bitcast.27, f32[1,1024]{1,0:T(1,128)} %get-tuple-element.42.gain, bf16[1024,1536]{1,0:T(8,128)(2,1)} %bitcast.25, bf16[512,1024]{1,0:T(8,128)(2,1)} %bitcast.31, ...), custom_call_target="tpu_custom_call" | custom-call | flops 1000000000 | bytes 8388608 | tf_op jit(solution)/shard_map/pallas_call | solution.py:296
  160.7 11.9 %shard_map.126 = bf16[4,64,1024]{2,1,0:T(8,128)(2,1)} custom-call(bf16[4,64,1024]{2,1,0:T(8,128)(2,1)} %bitcast.36), custom_call_target="tpu_custom_call" | custom-call | tf_op jit(solution)/shard_map/pallas_call | solution.py:276
  172.5 11.9 %shard_map.127 = bf16[4,64,1024]{2,1,0:T(8,128)(2,1)} custom-call(bf16[4,64,1024]{2,1,0:T(8,128)(2,1)} %bitcast.35), custom_call_target="tpu_custom_call" | custom-call | tf_op jit(solution)/shard_map/pallas_call | solution.py:276
  184.4 0.0 copy-start.1
  184.4 0.0 copy-start.3
  184.5 13.9 %shard_map.128 = (bf16[3,6,12,1024]{3,2,1,0:T(8,128)(2,1)}, f32[1,1024]{1,0:T(1,128)}, f32[8,1,1280]{2,1,0:T(1,128)}, bf16[3,6,12,1024]{3,2,1,0:T(8,128)(2,1)}) custom-call(bf16[256,1024]{1,0:T(8,128)(2,1)} %bitcast.33, bf16[256,1024]{1,0:T(8,128)(2,1)} %get-tuple-element.21.x_ref, f32[1,1024]{1,0:T(1,128)} %get-tuple-element.43.gain, ...), custom_call_target="tpu_custom_call" | custom-call | flops 1000000000 | bytes 8388608 | tf_op jit(solution)/shard_map/pallas_call | solution.py:296
  198.3 0.0 copy-done.1
  198.3 0.0 copy-done.3
  198.3 1.5 pad_maximum_fusion
  199.8 0.0 all-reduce.3.cloned.1.call-update
  199.8 118.3 %all-reduce.3.cloned.1.call-done = f32[1,22528]{1,0:T(1,128)} async-done(((f32[1,22528]{1,0:T(1,128)}), f32[1,22528]{1,0:T(1,128)}) %all-reduce.3.cloned.1.call-update) | async-done | bytes 90128 | tf_op jit(solution)/shard_map/psum | solution.py:366
  318.1 1.0 broadcast_multiply_fusion
  319.2 0.2 slice_reduce_fusion
  319.4 0.6 reshape.62
  320.0 0.7 reverse.1
  320.7 0.7 slice.50
  (2 shorter events, 0.0 us)
Async XLA Ops:
  7.2 5.3 %copy-start = (f32[2,8,1265]{2,1,0:T(8,128)S(1)}, f32[2,8,1265]{2,1,0:T(8,128)}, u32[]{:S(2)}) copy-start(f32[2,8,1265]{2,1,0:T(8,128)} %param.14) | copy-start | bytes 242884
  7.2 42.8 %all-gather.11.cloned.1.call-start = ((), (), s32[]{:S(2)}) async-start(), calls=%async_computation.2 | async-start | bytes 1179648 | tf_op jit(solution)/shard_map/all_gather | solution.py:310
  8.9 65.0 %all-gather.9.cloned.1.call-start = ((), (), s32[]{:S(2)}) async-start(), calls=%async_computation.1 | async-start | bytes 3538944 | tf_op jit(solution)/shard_map/all_gather | solution.py:309
  11.1 89.8 %all-gather.15.cloned.1.call-start = ((), (), s32[]{:S(2)}) async-start(), calls=%async_computation.4 | async-start | bytes 1179648 | tf_op jit(solution)/shard_map/all_gather | solution.py:310
  11.8 128.9 %all-gather.13.cloned.1.call-start = ((), (), s32[]{:S(2)}) async-start(), calls=%async_computation.3 | async-start | bytes 3538944 | tf_op jit(solution)/shard_map/all_gather | solution.py:309
  12.4 305.8 %all-reduce.3.cloned.1.call-start = ((), (), s32[]{:S(2)}) async-start(), calls=%async_computation | async-start | bytes 180224 | tf_op jit(solution)/shard_map/psum | solution.py:366
  14.7 30.0 %copy-start.2 = (f32[2,1024]{1,0:T(2,128)S(1)}, f32[2,1024]{1,0:T(2,128)}, u32[]{:S(2)}) copy-start(f32[2,1024]{1,0:T(2,128)} %param.13) | copy-start | bytes 24580
  184.4 13.9 %copy-start.1 = (f32[8,1,1280]{2,1,0:T(1,128)S(1)}, f32[8,1,1280]{2,1,0:T(1,128)}, u32[]{:S(2)}) copy-start(f32[8,1,1280]{2,1,0:T(1,128)} %get-tuple-element.35) | copy-start | bytes 122884
  184.4 13.9 %copy-start.3 = (f32[1,1024]{1,0:T(1,128)S(1)}, f32[1,1024]{1,0:T(1,128)}, u32[]{:S(2)}) copy-start(f32[1,1024]{1,0:T(1,128)} %get-tuple-element.33) | copy-start | bytes 12292
Sparse Core Ops, SparseCore 0:
  9.6 24.6 all-gather.10
  35.9 38.0 all-gather.8
  75.6 25.2 all-gather.14
  102.9 37.7 all-gather.12
  200.0 118.1 all-reduce.2

commit v2 on v1

--- a/solution.py
+++ b/solution.py
@@ -304,6 +304,197 @@
     )(*args)
 
 
+def shift_quads(field, ahead):
+    lats, lons = lax.axis_size("lat"), lax.axis_size("lon")
+    quads = field.reshape(4, QR, field.shape[-1])
+    sign = -1 if ahead else 1
+    arrived = []
+    for slot in range(4):
+        quad = 3 - slot
+        y, x = quad // 2, quad % 2
+        dy, dx = (1 - y, 1 - x) if ahead else (y, x)
+        if dy == 0 and dx == 0:
+            arrived.append(quads[quad])
+            continue
+        pairs = []
+        for lat in range(lats):
+            for lon in range(lons):
+                target = ((lat + sign * dy) % lats) * lons + (lon + sign * dx) % lons
+                pairs.append((lat * lons + lon, target))
+        arrived.append(lax.ppermute(quads[quad], ("lat", "lon"), pairs))
+    return jnp.concatenate(arrived, 0)
+
+
+def peers_of(axis):
+    me, size = lax.axis_index(axis), lax.axis_size(axis)
+    ahead = [(d, lax.rem(me + d, size)) for d in range(1, size)]
+    behind = [(d, lax.rem(me + size - d, size)) for d in range(1, size)]
+    return me, ahead, behind
+
+
+def greet(axes):
+    barrier = pltpu.get_barrier_semaphore()
+    count = 0
+    for axis in axes:
+        for _, peer in peers_of(axis)[1]:
+            pl.semaphore_signal(barrier, inc=1, device_id={axis: peer}, device_id_type=MESH)
+            count += 1
+    pl.semaphore_wait(barrier, count)
+
+
+def gather_kernel(w_in, w_proj, full_in, full_proj, send_z, recv_z, send_p, recv_p, send_c,
+                  recv_c, own):
+    dp, dp_ahead, _ = peers_of("dp")
+    lat, lat_ahead, _ = peers_of("lat")
+    lon, lon_ahead, lon_behind = peers_of("lon")
+    lons = lax.axis_size("lon")
+    arrays = ((w_in, full_in), (w_proj, full_proj))
+    mine = lat * lons + lon
+    greet(("dp", "lat", "lon"))
+    sent = []
+
+    def put(src, dst, send, recv, device):
+        copy = pltpu.make_async_remote_copy(
+            src_ref=src, dst_ref=dst, send_sem=send, recv_sem=recv, device_id=device,
+            device_id_type=MESH,
+        )
+        copy.start()
+        sent.append(copy)
+        return copy
+
+    along = {}
+    for d, peer in lon_ahead:
+        for n, (part, full) in enumerate(arrays):
+            along[d, n] = put(part.at[0, dp], full.at[mine, dp], send_z.at[n, d], recv_z.at[n, d],
+                              {"lon": peer})
+    local = []
+    across = []
+    for n, (part, full) in enumerate(arrays):
+        local.append(pltpu.make_async_copy(part.at[0], full.at[mine], own.at[n]))
+        local[-1].start()
+        for f, peer in lat_ahead:
+            across.append(put(part.at[0], full.at[mine], send_c.at[n, 0, f], recv_c.at[n, 0, f],
+                              {"lat": peer}))
+    plane = {}
+    for d, source in lon_behind:
+        shard = lat * lons + source
+        for n, (_, full) in enumerate(arrays):
+            along[d, n].wait_recv()
+            for e, peer in dp_ahead:
+                plane[d, n, e] = put(full.at[shard, dp], full.at[shard, dp], send_p.at[n, d, e],
+                                     recv_p.at[n, d, e], {"dp": peer})
+    for d, source in lon_behind:
+        shard = lat * lons + source
+        for n, (_, full) in enumerate(arrays):
+            for e, _ in dp_ahead:
+                plane[d, n, e].wait_recv()
+            for f, peer in lat_ahead:
+                across.append(put(full.at[shard], full.at[shard], send_c.at[n, d, f],
+                                  recv_c.at[n, d, f], {"lat": peer}))
+    for copy in local:
+        copy.wait()
+    for copy in across:
+        copy.wait_recv()
+    for copy in sent:
+        copy.wait_send()
+
+
+def fetch_first(w_qkv, w_out):
+    dps, lats, lons = (lax.axis_size(axis) for axis in ("dp", "lat", "lon"))
+    shards = lats * lons
+    if w_qkv.shape[1] % (16 * dps) or w_out.shape[1] % (16 * dps):
+        return fetch_block(w_qkv, w_out, 0)
+    parts = [w.reshape(2, dps, w.shape[1] // dps, w.shape[2]) for w in (w_qkv, w_out)]
+    dma = pltpu.SemaphoreType.DMA
+    full = pl.pallas_call(
+        gather_kernel,
+        out_shape=[
+            jax.ShapeDtypeStruct((shards,) + part.shape[1:], part.dtype) for part in parts
+        ],
+        in_specs=[pl.BlockSpec(memory_space=pltpu.VMEM)] * 2,
+        out_specs=[pl.BlockSpec(memory_space=pltpu.VMEM)] * 2,
+        scratch_shapes=[
+            dma((2, lons)), dma((2, lons)), dma((2, lons, dps)), dma((2, lons, dps)),
+            dma((2, lons, lats)), dma((2, lons, lats)), dma((2,)),
+        ],
+        compiler_params=pltpu.CompilerParams(
+            collective_id=5, has_side_effects=True, vmem_limit_bytes=VMEM_LIMIT
+        ),
+    )(*parts)
+    return tuple(array.reshape(-1, array.shape[-1]) for array in full)
+
+
+def reduce_kernel(data, total, from_lat, lat_sum, from_dp, from_lon, lat_all, send, recv):
+    dp, dp_ahead, dp_behind = peers_of("dp")
+    lat, lat_ahead, lat_behind = peers_of("lat")
+    lon, lon_ahead, _ = peers_of("lon")
+    lons = lax.axis_size("lon")
+    greet(("dp", "lat", "lon"))
+    sent = []
+
+    def swap(phase, axis, ahead, pick, place):
+        copies = []
+        for d, peer in ahead:
+            copies.append(
+                pltpu.make_async_remote_copy(
+                    src_ref=pick(peer), dst_ref=place, send_sem=send.at[phase, d],
+                    recv_sem=recv.at[phase, d], device_id={axis: peer}, device_id_type=MESH,
+                )
+            )
+            copies[-1].start()
+        for copy in copies:
+            copy.wait_recv()
+        sent.extend(copies)
+
+    swap(0, "lat", lat_ahead, lambda peer: data.at[peer], from_lat.at[lat])
+    value = data[lat]
+    for _, peer in lat_behind:
+        value = value + from_lat[peer]
+    lat_sum[...] = value
+    swap(1, "dp", dp_ahead, lambda peer: lat_sum.at[peer], from_dp.at[dp])
+    value = lat_sum[dp]
+    for _, peer in dp_behind:
+        value = value + from_dp[peer]
+    from_lon[lon] = value
+    swap(2, "lon", lon_ahead, lambda peer: from_lon.at[lon], from_lon.at[lon])
+    value = from_lon[0]
+    for n in range(1, lons):
+        value = value + from_lon[n]
+    lat_all[dp] = value
+    swap(3, "dp", dp_ahead, lambda peer: lat_all.at[dp], lat_all.at[dp])
+    total[lat] = lat_all[...]
+    swap(4, "lat", lat_ahead, lambda peer: lat_all, total.at[lat])
+    for copy in sent:
+        copy.wait_send()
+
+
+def sum_all(packed):
+    dps, lats, lons = (lax.axis_size(axis) for axis in ("dp", "lat", "lon"))
+    length = packed.shape[1]
+    rows = -(-length // (128 * 8 * dps * lats)) * 8
+    padded = jnp.pad(packed[0], (0, rows * 128 * dps * lats - length))
+    most = max(dps, lats, lons)
+    f32 = jnp.float32
+    piece = (rows, 128)
+    total = pl.pallas_call(
+        reduce_kernel,
+        out_shape=jax.ShapeDtypeStruct((lats, dps) + piece, f32),
+        in_specs=[pl.BlockSpec(memory_space=pltpu.VMEM)],
+        out_specs=pl.BlockSpec(memory_space=pltpu.VMEM),
+        scratch_shapes=[
+            pltpu.VMEM((lats, dps) + piece, f32),
+            pltpu.VMEM((dps,) + piece, f32),
+            pltpu.VMEM((dps,) + piece, f32),
+            pltpu.VMEM((lons,) + piece, f32),
+            pltpu.VMEM((dps,) + piece, f32),
+            pltpu.SemaphoreType.DMA((5, most)),
+            pltpu.SemaphoreType.DMA((5, most)),
+        ],
+        compiler_params=pltpu.CompilerParams(collective_id=6, has_side_effects=True),
+    )(padded.reshape((lats, dps) + piece))
+    return total.reshape(1, -1)[:, :length]
+
+
 def fetch_block(w_qkv, w_out, index):
     return (
         lax.all_gather(w_qkv[index], ("lat", "lon"), axis=0, tiled=True),
@@ -318,7 +509,7 @@
     order = jnp.asarray(order_matrix(), bf)
     spread = jnp.asarray(spread_matrix(), bf)
     collect = jnp.asarray(spread_matrix().T.copy(), bf)
-    in_one, proj_one = fetch_block(w_qkv, w_out, 0)
+    in_one, proj_one = fetch_first(w_qkv, w_out)
     in_two, proj_two = fetch_block(w_qkv, w_out, 1)
     polar = lax.axis_index("lat") == lax.axis_size("lat") - 1
     flag = jnp.where(polar, 1, 0).astype(jnp.int32).reshape(1)
@@ -334,7 +525,7 @@
     )
     saved = [((ROWS, 3 * inner), bf), ((H, ROWS, ROWS), bf)]
     wide = [((ROWS, inner), bf)]
-    g_two = exchange(g_out, True, 0)
+    g_two = shift_quads(g_out, True)
     gain_one, gain_two = gains[0:1], gains[1:2]
     first, qkv_one, probs_one = call(
         forward_kernel, [field] + saved, wide, (x_one, gain_one, in_one, proj_one, bias[:H])
@@ -343,7 +534,7 @@
     second, qkv_two, probs_two = call(
         forward_kernel, [field] + saved, wide, (x_two, gain_two, in_two, proj_two, bias[H:])
     )
-    y_back = exchange(second, False, 2)
+    y_back = shift_quads(second, False)
     back = [((ROWS, inner), bf), ((ROWS, 3 * inner), bf), ((H, ROWS, SPAN), f32)]
     terms = [((1, features), f32), ((H, 1, TABLE), f32)]
     gx_two, gterm_two, tterm_two = call(
@@ -363,7 +554,7 @@
     packed = jnp.concatenate(
         [gterm_one, gterm_two, tterm_one.reshape(1, -1), tterm_two.reshape(1, -1)], 1
     )
-    packed = lax.psum(packed, ("dp", "lat", "lon"))
+    packed = sum_all(packed)
     total = math.prod(tokens.shape[:4]) * math.prod(
         lax.axis_size(axis) for axis in ("dp", "lat", "lon")
     )

time: 329 us -> 183 us (0.56)
  waiting for transfers between devices: 187 us -> 0.09 us
  Pallas kernels: 111 us -> 140 us
  starting transfers between devices: 0.2 us -> 7.85 us
  local copies, waits for them, and re-layouts: 13.6 us -> 17 us
    psum x1 -> x0, waiting for transfers between devices: 118 us -> none  [on_device(): packed = lax.psum(packed, ('dp', 'lat', 'lon'))]
    all_gather x2 -> x1, waiting for transfers between devices: 63.8 us -> 0.02 us  [fetch_block(): lax.all_gather(w_qkv[index], ('lat', 'lon'), axis=0, tiled=True)]
    pallas_call x0 -> x2, Pallas kernels: none -> 48.6 us  [the longest x1 32.9 us: fetch_first(): pl.pallas_call(gather_kernel, out_shape=[jax.ShapeDtypeStruct((shards,) +...]
    pallas_call x4 -> x2, Pallas kernels: 53.9 us -> 34 us  [exchange(): pl.pallas_call(functools.partial(exchange_kernel, ahead), out_shape=jax.S...]
    ppermute x0 -> x6, starting transfers between devices: none -> 7.77 us  [shift_quads(): arrived.append(lax.ppermute(quads[quad], ('lat', 'lon'), pairs))]
  transfers between devices with their start and end apart: 5 -> 8, of which waited for: 4 -> 0; matrix products, arithmetic and copies ran while one was open for 3% -> 7% of each run, Pallas kernels for 16% -> 60%
where the time goes in v2:
time: 183 us
  Pallas kernels  140 us (77%)
  local copies, waits for them, and re-layouts  17 us (9%)
  between operations  14.2 us (8%)
  starting transfers between devices  7.85 us (4%)
  other arithmetic  3.52 us (2%)
    pallas_call x5, Pallas kernels, call(): pl.pallas_call(kernel, out_shape=[jax.ShapeDtypeStruct(shape, dtype) for...  57.3 us
    pallas_call x2, Pallas kernels, exchange(): pl.pallas_call(functools.partial(exchange_kernel, ahead), out_shape=jax.S...  34 us
    pallas_call x1, Pallas kernels, fetch_first(): pl.pallas_call(gather_kernel, out_shape=[jax.ShapeDtypeStruct((shards,) +...  32.9 us
    pallas_call x1, Pallas kernels, sum_all(): pl.pallas_call(reduce_kernel, out_shape=jax.ShapeDtypeStruct((lats, dps)...  15.7 us
    ppermute x6, starting transfers between devices, shift_quads(): arrived.append(lax.ppermute(quads[quad], ('lat', 'lon'), pairs))  7.77 us
    slice x1, local copies, waits for them, and re-layouts, on_device(): bias[H:]  4.75 us
  transfers between devices with their start and end apart: 8, of which 0 were waited for; matrix products, arithmetic and copies ran while one was open for 7% of the time, Pallas kernels for 60%

profile of v2, /device:TPU:0, one launch (start us, length us, event | category | flops | bytes accessed | tf_op | source)
XLA Modules:
  0.0 182.5 jit_solution(7661143783986269212)
XLA Ops:
  7.2 0.0 all-gather.7.cloned.1.call-start
  7.2 1.6 slice.70
  8.8 0.0 all-gather.7.cloned.1.call-update
  8.8 0.0 all-gather.5.cloned.1.call-start
  8.8 1.8 slice.69
  10.6 0.0 all-gather.5.cloned.1.call-update
  10.6 1.0 reshape.74
  11.6 1.2 reverse
  12.8 0.2 slice.87
  13.1 0.7 pad.8.tab
  13.8 0.0 copy-start.1
  13.8 16.9 %shard_map.120 = (bf16[256,1024]{1,0:T(8,128)(2,1)}, bf16[256,1024]{1,0:T(8,128)(2,1)}, f32[16,256,256]{2,1,0:T(8,128)}) custom-call(bf16[3,6,12,1024]{3,2,1,0:T(8,128)(2,1)} %bitcast.44, bf16[3,6,12,1024]{3,2,1,0:T(8,128)(2,1)} %bitcast.45, f32[16,1,1280]{2,1,0:T(1,128)} %pad.8.tab, bf16[256,288]{1,0:T(8,128)(2,1)} %constant.20.clone.order, ...), custom_call_target="tpu_custom_call" | custom-call | flops 8000000000 | bytes 8388608 | tf_op jit(solution)/shard_map/pallas_call | solution.py:296
  30.7 1.1 fusion.2
  31.8 4.5 %collective-permute-start.2 = (bf16[64,1024]{1,0:T(8,128)(2,1)S(1)}, bf16[64,1024]{1,0:T(8,128)(2,1)S(1)}, u32[]{:S(2)}, u32[]{:S(2)}) collective-permute-start(bf16[64,1024]{1,0:T(8,128)(2,1)S(1)} %get-tuple-element.47), channel_id=1, source_target_pairs={{0,7},{1,4},{2,5},{3,6},{4,3},{5,0},{6,1},{7,2},{8,15},{9,12},{10,... | collective-permute-start | bytes 393224 | tf_op jit(solution)/shard_map/ppermute | solution.py:324
  36.4 0.7 collective-permute-start.1
  37.0 0.5 collective-permute-start
  37.5 32.9 %shard_map.121 = (bf16[8,4,32,1536]{3,2,1,0:T(8,128)(2,1)}, bf16[8,4,16,1024]{3,2,1,0:T(8,128)(2,1)}) custom-call(bf16[2,4,32,1536]{3,2,1,0:T(8,128)(2,1)} %bitcast.34, bf16[2,4,16,1024]{3,2,1,0:T(8,128)(2,1)} %bitcast.35), custom_call_target="tpu_custom_call" | custom-call | tf_op jit(solution)/shard_map/pallas_call | solution.py:409
  70.4 0.0 copy-done.1
  70.4 0.6 fusion.3
  71.0 4.7 %fusion = (f32[8,256,256]{2,1,0:T(8,128)}, f32[8,256,256]{2,1,0:T(8,128)}) fusion(f32[16,256,256]{2,1,0:T(8,128)} %get-tuple-element.26), kind=kLoop, calls=%fused_computation.6 | loop fusion | bytes 8388608 | tf_op jit(solution)/shard_map/slice | solution.py:535
  75.7 6.7 %shard_map.122 = (bf16[256,1024]{1,0:T(8,128)(2,1)}, bf16[256,1536]{1,0:T(8,128)(2,1)}, bf16[8,256,256]{2,1,0:T(8,128)(2,1)}) custom-call(bf16[256,1024]{1,0:T(8,128)(2,1)} %get-tuple-element.23.x_ref, f32[1,1024]{1,0:T(1,128)} %get-tuple-element.51.gain, bf16[1024,1536]{1,0:T(8,128)(2,1)} %bitcast.23, bf16[512,1024]{1,0:T(8,128)(2,1)} %bitcast.31, ...), custom_call_target="tpu_custom_call" | custom-call | flops 1000000000 | bytes 8388608 | tf_op jit(solution)/shard_map/pallas_call | solution.py:296
  82.4 22.1 %shard_map.123 = bf16[4,64,1024]{2,1,0:T(8,128)(2,1)} custom-call(bf16[4,64,1024]{2,1,0:T(8,128)(2,1)} %bitcast.37), custom_call_target="tpu_custom_call" | custom-call | tf_op jit(solution)/shard_map/pallas_call | solution.py:276
  104.6 0.0 all-gather.7.cloned.1.call-done
  104.6 0.0 all-gather.5.cloned.1.call-done
  104.6 6.7 %shard_map.124 = (bf16[256,1024]{1,0:T(8,128)(2,1)}, bf16[256,1536]{1,0:T(8,128)(2,1)}, bf16[8,256,256]{2,1,0:T(8,128)(2,1)}) custom-call(bf16[256,1024]{1,0:T(8,128)(2,1)} %bitcast.27, f32[1,1024]{1,0:T(1,128)} %get-tuple-element.50.gain, bf16[1024,1536]{1,0:T(8,128)(2,1)} %bitcast.25, bf16[512,1024]{1,0:T(8,128)(2,1)} %bitcast.29, ...), custom_call_target="tpu_custom_call" | custom-call | flops 1000000000 | bytes 8388608 | tf_op jit(solution)/shard_map/pallas_call | solution.py:296
  111.3 1.1 fusion.1
  112.4 0.1 collective-permute-start.5
  112.5 0.1 collective-permute-start.4
  112.6 0.0 collective-permute-done.2
  112.6 2.0 %collective-permute-start.3 = (bf16[64,1024]{1,0:T(8,128)(2,1)S(1)}, bf16[64,1024]{1,0:T(8,128)(2,1)S(1)}, u32[]{:S(2)}, u32[]{:S(2)}) collective-permute-start(bf16[64,1024]{1,0:T(8,128)(2,1)S(1)} %get-tuple-element.42), channel_id=1, source_target_pairs={{0,5},{1,6},{2,7},{3,4},{4,1},{5,2},{6,3},{7,0},{8,13},{9,14},{10,... | collective-permute-start | bytes 393224 | tf_op jit(solution)/shard_map/ppermute | solution.py:324
  114.5 0.0 collective-permute-done.1
  114.6 0.0 collective-permute-done
  114.6 0.8 pad_maximum_fusion.g_ref
  115.4 13.1 %shard_map.125 = (bf16[256,1024]{1,0:T(8,128)(2,1)}, f32[1,1024]{1,0:T(1,128)}, f32[8,1,1280]{2,1,0:T(1,128)}) custom-call(bf16[256,1024]{1,0:T(8,128)(2,1)} %pad_maximum_fusion.g_ref, bf16[256,1024]{1,0:T(8,128)(2,1)} %bitcast.28, f32[1,1024]{1,0:T(1,128)} %get-tuple-element.50.gain, bf16[1024,1536]{1,0:T(8,128)(2,1)} %bitcast.26, ...), custom_call_target="tpu_custom_call" | custom-call | flops 1000000000 | bytes 8388608 | tf_op jit(solution)/shard_map/pallas_call | solution.py:296
  128.5 11.9 %shard_map.126 = bf16[4,64,1024]{2,1,0:T(8,128)(2,1)} custom-call(bf16[4,64,1024]{2,1,0:T(8,128)(2,1)} %bitcast.36), custom_call_target="tpu_custom_call" | custom-call | tf_op jit(solution)/shard_map/pallas_call | solution.py:276
  140.4 0.0 collective-permute-done.5
  140.4 0.0 collective-permute-done.4
  140.4 0.0 collective-permute-done.3
  140.4 0.8 pad_maximum_fusion.1.y_ref
  141.3 0.0 copy-start
  141.3 0.0 copy-start.2
  141.3 13.9 %shard_map.127 = (bf16[3,6,12,1024]{3,2,1,0:T(8,128)(2,1)}, f32[1,1024]{1,0:T(1,128)}, f32[8,1,1280]{2,1,0:T(1,128)}, bf16[3,6,12,1024]{3,2,1,0:T(8,128)(2,1)}) custom-call(bf16[256,1024]{1,0:T(8,128)(2,1)} %bitcast.33, bf16[256,1024]{1,0:T(8,128)(2,1)} %get-tuple-element.23.x_ref, f32[1,1024]{1,0:T(1,128)} %get-tuple-element.51.gain, ...), custom_call_target="tpu_custom_call" | custom-call | flops 1000000000 | bytes 8388608 | tf_op jit(solution)/shard_map/pallas_call | solution.py:296
  155.1 0.0 copy-done
  155.1 0.0 copy-done.2
  155.1 0.9 pad_maximum_fusion.2
  156.0 0.6 pad.9
  156.7 15.7 %shard_map.128 = f32[2,4,24,128]{3,2,1,0:T(8,128)} custom-call(f32[2,4,24,128]{3,2,1,0:T(8,128)} %bitcast.38), custom_call_target="tpu_custom_call" | custom-call | tf_op jit(solution)/shard_map/pallas_call | solution.py:479
  172.3 1.0 slice_multiply_fusion
  173.4 0.2 slice_reduce_fusion
  173.6 0.6 reshape.88
  174.2 0.7 reverse.1
  174.9 0.7 slice.88
  (2 shorter events, 0.0 us)
Async XLA Ops:
  7.2 97.4 %all-gather.7.cloned.1.call-start = ((), (), s32[]{:S(2)}) async-start(), calls=%async_computation.1 | async-start | bytes 1179648 | tf_op jit(solution)/shard_map/all_gather | solution.py:501
  8.8 95.8 %all-gather.5.cloned.1.call-start = ((), (), s32[]{:S(2)}) async-start(), calls=%async_computation | async-start | bytes 3538944 | tf_op jit(solution)/shard_map/all_gather | solution.py:500
  13.8 56.6 %copy-start.1 = (f32[2,1024]{1,0:T(2,128)S(1)}, f32[2,1024]{1,0:T(2,128)}, u32[]{:S(2)}) copy-start(f32[2,1024]{1,0:T(2,128)} %param.13) | copy-start | bytes 24580
  31.8 80.8 %collective-permute-start.2 = (bf16[64,1024]{1,0:T(8,128)(2,1)S(1)}, bf16[64,1024]{1,0:T(8,128)(2,1)S(1)}, u32[]{:S(2)}, u32[]{:S(2)}) collective-permute-start(bf16[64,1024]{1,0:T(8,128)(2,1)S(1)} %get-tuple-element.47), channel_id=1, source_target_pairs={{0,7},{1,4},{2,5},{3,6},{4,3},{5,0},{6,1},{7,2},{8,15},{9,12},{10,... | collective-permute-start | bytes 393224 | tf_op jit(solution)/shard_map/ppermute | solution.py:324
  36.4 78.2 %collective-permute-start.1 = (bf16[64,1024]{1,0:T(8,128)(2,1)S(1)}, bf16[64,1024]{1,0:T(8,128)(2,1)S(1)}, u32[]{:S(2)}, u32[]{:S(2)}) collective-permute-start(bf16[64,1024]{1,0:T(8,128)(2,1)S(1)} %get-tuple-element.48), channel_id=1, source_target_pairs={{0,4},{1,5},{2,6},{3,7},{4,0},{5,1},{6,2},{7,3},{8,12},{9,13},{10,... | collective-permute-start | bytes 393224 | tf_op jit(solution)/shard_map/ppermute | solution.py:324
  37.0 77.5 %collective-permute-start = (bf16[64,1024]{1,0:T(8,128)(2,1)S(1)}, bf16[64,1024]{1,0:T(8,128)(2,1)S(1)}, u32[]{:S(2)}, u32[]{:S(2)}) collective-permute-start(bf16[64,1024]{1,0:T(8,128)(2,1)S(1)} %get-tuple-element.49), channel_id=1, source_target_pairs={{0,3},{1,0},{2,1},{3,2},{4,7},{5,4},{6,5},{7,6},{8,11},{9,8},{10,9... | collective-permute-start | bytes 393224 | tf_op jit(solution)/shard_map/ppermute | solution.py:324
  112.4 28.0 %collective-permute-start.5 = (bf16[64,1024]{1,0:T(8,128)(2,1)S(1)}, bf16[64,1024]{1,0:T(8,128)(2,1)S(1)}, u32[]{:S(2)}, u32[]{:S(2)}) collective-permute-start(bf16[64,1024]{1,0:T(8,128)(2,1)S(1)} %get-tuple-element.44), channel_id=1, source_target_pairs={{0,1},{1,2},{2,3},{3,0},{4,5},{5,6},{6,7},{7,4},{8,9},{9,10},{10,1... | collective-permute-start | bytes 393224 | tf_op jit(solution)/shard_map/ppermute | solution.py:324
  112.5 27.9 %collective-permute-start.4 = (bf16[64,1024]{1,0:T(8,128)(2,1)S(1)}, bf16[64,1024]{1,0:T(8,128)(2,1)S(1)}, u32[]{:S(2)}, u32[]{:S(2)}) collective-permute-start(bf16[64,1024]{1,0:T(8,128)(2,1)S(1)} %get-tuple-element.45), channel_id=1, source_target_pairs={{0,4},{1,5},{2,6},{3,7},{4,0},{5,1},{6,2},{7,3},{8,12},{9,13},{10,... | collective-permute-start | bytes 393224 | tf_op jit(solution)/shard_map/ppermute | solution.py:324
  112.6 27.8 %collective-permute-start.3 = (bf16[64,1024]{1,0:T(8,128)(2,1)S(1)}, bf16[64,1024]{1,0:T(8,128)(2,1)S(1)}, u32[]{:S(2)}, u32[]{:S(2)}) collective-permute-start(bf16[64,1024]{1,0:T(8,128)(2,1)S(1)} %get-tuple-element.42), channel_id=1, source_target_pairs={{0,5},{1,6},{2,7},{3,4},{4,1},{5,2},{6,3},{7,0},{8,13},{9,14},{10,... | collective-permute-start | bytes 393224 | tf_op jit(solution)/shard_map/ppermute | solution.py:324
  141.3 13.9 %copy-start = (f32[8,1,1280]{2,1,0:T(1,128)S(1)}, f32[8,1,1280]{2,1,0:T(1,128)}, u32[]{:S(2)}) copy-start(f32[8,1,1280]{2,1,0:T(1,128)} %get-tuple-element.39) | copy-start | bytes 122884
  141.3 13.9 %copy-start.2 = (f32[1,1024]{1,0:T(1,128)S(1)}, f32[1,1024]{1,0:T(1,128)}, u32[]{:S(2)}) copy-start(f32[1,1024]{1,0:T(1,128)} %get-tuple-element.37) | copy-start | bytes 12292
Sparse Core Ops, SparseCore 0:
  9.6 24.8 all-gather.6
  36.6 43.4 all-gather.4

commit v3 on v2

--- a/solution.py
+++ b/solution.py
@@ -87,22 +87,27 @@
     return lax.dot_general(a, b, (((0,), (0,)), ((), ())), preferred_element_type=jnp.float32)
 
 
-def prep_kernel(tok, cot, tab, order, spread, flag, x_out, g_out, bias_out, lines, rows):
-    lines[...] = jnp.zeros_like(lines)
-    for source, target in ((tok, x_out), (cot, g_out)):
-        for k in range(LINES):
-            lines[k, 0:WW, :] = source[k // WH, k % WH]
-        flat = lines[...].reshape(LINES * LINE, lines.shape[2])
-        target[...] = dot(order[...], flat).astype(jnp.bfloat16)
-    rows[...] = jnp.zeros_like(rows)
+STAGES = (5, 11, 2 * H)
+
+
+def prep_stage(stage, tok, cot, tab, order, spread, x_out, g_out, bias_one, bias_two, lines, rows):
+    if stage == 0:
+        lines[...] = jnp.zeros_like(lines)
+        for source, target in ((tok, x_out), (cot, g_out)):
+            for k in range(LINES):
+                lines[k, 0:WW, :] = source[k // WH, k % WH]
+            flat = lines[...].reshape(LINES * LINE, lines.shape[2])
+            target[...] = dot(order[...], flat).astype(jnp.bfloat16)
+        rows[...] = jnp.zeros_like(rows)
     key = lax.broadcasted_iota(jnp.int32, (ROWS, ROWS), 1)
     query = lax.broadcasted_iota(jnp.int32, (ROWS, ROWS), 0)
     pad = key % QR >= GROUPS * SW
-    apart = (key // (2 * QR)) != (query // (2 * QR))
-    drop_two = pad | (apart & (flag[0] == 1))
-
-    def one_head(n, carry):
-        base = jnp.broadcast_to(tab[n], (8, TABLE))
+    polar = jnp.where(lax.axis_index("lat") == lax.axis_size("lat") - 1, 1, 0)
+    apart = jnp.where((key // (2 * QR)) != (query // (2 * QR)), polar, 0)
+    drops = (pad, pad | (apart == 1))
+
+    def one_head(block, target, n, carry):
+        base = jnp.broadcast_to(tab[block * H + n], (8, TABLE))
         base = pltpu.roll(base, 0, 1, stride=1, stride_axis=0)
         for row, shift in group_list():
             rows[row : row + SW, :] = pltpu.roll(base, TABLE - shift, 1)[:SW, :SPAN]
@@ -113,17 +118,20 @@
         low = (rest - mid.astype(jnp.float32)).astype(jnp.bfloat16)
         part = spread[...]
         bias = dot(high, part) + dot(mid, part) + dot(low, part)
-        bias_out[n] = bias
+        target[n] = jnp.where(drops[block], FAR, bias)
         return carry
 
-    lax.fori_loop(0, 2 * H, one_head, 0)
-
-    def mask_head(n, carry):
-        bias_out[n] = jnp.where(pad, FAR, bias_out[n])
-        bias_out[n + H] = jnp.where(drop_two, FAR, bias_out[n + H])
-        return carry
-
-    lax.fori_loop(0, H, mask_head, 0)
+    first = 0 if stage == 0 else STAGES[stage - 1]
+    last = STAGES[stage]
+    for block, target in ((0, bias_one), (1, bias_two)):
+        low, high = max(first - block * H, 0), min(last - block * H, H)
+        if low < high:
+            lax.fori_loop(low, high, functools.partial(one_head, block, target), 0)
+
+
+def prep_kernel(*refs):
+    for stage in range(len(STAGES)):
+        prep_stage(stage, *refs)
 
 
 def normalise(values):
@@ -342,8 +350,12 @@
     pl.semaphore_wait(barrier, count)
 
 
-def gather_kernel(w_in, w_proj, full_in, full_proj, send_z, recv_z, send_p, recv_p, send_c,
+def gather_kernel(w_in, w_proj, tok, cot, tab, order, spread, full_in, full_proj, x_out, g_out,
+                  bias_one, bias_two, lines, rows, send_z, recv_z, send_p, recv_p, send_c,
                   recv_c, own):
+    prep = functools.partial(prep_stage, tok=tok, cot=cot, tab=tab, order=order, spread=spread,
+                             x_out=x_out, g_out=g_out, bias_one=bias_one, bias_two=bias_two,
+                             lines=lines, rows=rows)
     dp, dp_ahead, _ = peers_of("dp")
     lat, lat_ahead, _ = peers_of("lat")
     lon, lon_ahead, lon_behind = peers_of("lon")
@@ -375,6 +387,7 @@
         for f, peer in lat_ahead:
             across.append(put(part.at[0], full.at[mine], send_c.at[n, 0, f], recv_c.at[n, 0, f],
                               {"lat": peer}))
+    prep(0)
     plane = {}
     for d, source in lon_behind:
         shard = lat * lons + source
@@ -383,6 +396,7 @@
             for e, peer in dp_ahead:
                 plane[d, n, e] = put(full.at[shard, dp], full.at[shard, dp], send_p.at[n, d, e],
                                      recv_p.at[n, d, e], {"dp": peer})
+    prep(1)
     for d, source in lon_behind:
         shard = lat * lons + source
         for n, (_, full) in enumerate(arrays):
@@ -391,6 +405,7 @@
             for f, peer in lat_ahead:
                 across.append(put(full.at[shard], full.at[shard], send_c.at[n, d, f],
                                   recv_c.at[n, d, f], {"lat": peer}))
+    prep(2)
     for copy in local:
         copy.wait()
     for copy in across:
@@ -399,71 +414,96 @@
         copy.wait_send()
 
 
-def fetch_first(w_qkv, w_out):
+def fetch_first(w_qkv, w_out, prep_args, prep_out, prep_scratch):
     dps, lats, lons = (lax.axis_size(axis) for axis in ("dp", "lat", "lon"))
     shards = lats * lons
     if w_qkv.shape[1] % (16 * dps) or w_out.shape[1] % (16 * dps):
-        return fetch_block(w_qkv, w_out, 0)
+        full = fetch_block(w_qkv, w_out, 0)
+        return full, call(prep_kernel, prep_out, prep_scratch, prep_args, flops=8 * 10**9)
     parts = [w.reshape(2, dps, w.shape[1] // dps, w.shape[2]) for w in (w_qkv, w_out)]
     dma = pltpu.SemaphoreType.DMA
-    full = pl.pallas_call(
+    shapes = [((shards,) + part.shape[1:], part.dtype) for part in parts] + prep_out
+    vmem = pl.BlockSpec(memory_space=pltpu.VMEM)
+    found = pl.pallas_call(
         gather_kernel,
-        out_shape=[
-            jax.ShapeDtypeStruct((shards,) + part.shape[1:], part.dtype) for part in parts
-        ],
-        in_specs=[pl.BlockSpec(memory_space=pltpu.VMEM)] * 2,
-        out_specs=[pl.BlockSpec(memory_space=pltpu.VMEM)] * 2,
-        scratch_shapes=[
+        out_shape=[jax.ShapeDtypeStruct(shape, dtype) for shape, dtype in shapes],
+        in_specs=[vmem] * (2 + len(prep_args)),
+        out_specs=[vmem] * len(shapes),
+        scratch_shapes=[pltpu.VMEM(shape, dtype) for shape, dtype in prep_scratch]
+        + [
             dma((2, lons)), dma((2, lons)), dma((2, lons, dps)), dma((2, lons, dps)),
             dma((2, lons, lats)), dma((2, lons, lats)), dma((2,)),
         ],
         compiler_params=pltpu.CompilerParams(
             collective_id=5, has_side_effects=True, vmem_limit_bytes=VMEM_LIMIT
         ),
-    )(*parts)
-    return tuple(array.reshape(-1, array.shape[-1]) for array in full)
-
-
-def reduce_kernel(data, total, from_lat, lat_sum, from_dp, from_lon, lat_all, send, recv):
-    dp, dp_ahead, dp_behind = peers_of("dp")
-    lat, lat_ahead, lat_behind = peers_of("lat")
+    )(*parts, *prep_args)
+    return tuple(array.reshape(-1, array.shape[-1]) for array in found[:2]), found[2:]
+
+
+def plane_peers():
+    dps, lats = lax.axis_size("dp"), lax.axis_size("lat")
+    dp, lat = lax.axis_index("dp"), lax.axis_index("lat")
+    ahead, behind = [], []
+    for far in range(1, dps * lats):
+        a, b = far // dps, far % dps
+        ahead.append((far, lax.rem(lat + a, lats), lax.rem(dp + b, dps)))
+        behind.append((far, lax.rem(lat + lats - a, lats), lax.rem(dp + dps - b, dps)))
+    return ahead, behind
+
+
+def reduce_kernel(data, total, from_plane, from_lon, send, recv, send_z, recv_z):
+    dp, lat = lax.axis_index("dp"), lax.axis_index("lat")
+    ahead, behind = plane_peers()
     lon, lon_ahead, _ = peers_of("lon")
     lons = lax.axis_size("lon")
-    greet(("dp", "lat", "lon"))
+    barrier = pltpu.get_barrier_semaphore()
+    for _, a, b in ahead:
+        pl.semaphore_signal(
+            barrier, inc=1, device_id={"lat": a, "dp": b}, device_id_type=MESH
+        )
+    for _, peer in lon_ahead:
+        pl.semaphore_signal(barrier, inc=1, device_id={"lon": peer}, device_id_type=MESH)
+    pl.semaphore_wait(barrier, len(ahead) + len(lon_ahead))
     sent = []
 
-    def swap(phase, axis, ahead, pick, place):
-        copies = []
-        for d, peer in ahead:
-            copies.append(
-                pltpu.make_async_remote_copy(
-                    src_ref=pick(peer), dst_ref=place, send_sem=send.at[phase, d],
-                    recv_sem=recv.at[phase, d], device_id={axis: peer}, device_id_type=MESH,
-                )
-            )
-            copies[-1].start()
-        for copy in copies:
-            copy.wait_recv()
-        sent.extend(copies)
-
-    swap(0, "lat", lat_ahead, lambda peer: data.at[peer], from_lat.at[lat])
-    value = data[lat]
-    for _, peer in lat_behind:
-        value = value + from_lat[peer]
-    lat_sum[...] = value
-    swap(1, "dp", dp_ahead, lambda peer: lat_sum.at[peer], from_dp.at[dp])
-    value = lat_sum[dp]
-    for _, peer in dp_behind:
-        value = value + from_dp[peer]
+    def put(src, dst, send_sem, recv_sem, device):
+        copy = pltpu.make_async_remote_copy(
+            src_ref=src, dst_ref=dst, send_sem=send_sem, recv_sem=recv_sem, device_id=device,
+            device_id_type=MESH,
+        )
+        copy.start()
+        sent.append(copy)
+        return copy
+
+    first = [
+        put(data.at[a, b], from_plane.at[lat, dp], send.at[0, d], recv.at[0, d],
+            {"lat": a, "dp": b})
+        for d, a, b in ahead
+    ]
+    value = data[lat, dp]
+    for copy in first:
+        copy.wait_recv()
+    for _, a, b in behind:
+        value = value + from_plane[a, b]
     from_lon[lon] = value
-    swap(2, "lon", lon_ahead, lambda peer: from_lon.at[lon], from_lon.at[lon])
+    second = [
+        put(from_lon.at[lon], from_lon.at[lon], send_z.at[d], recv_z.at[d], {"lon": peer})
+        for d, peer in lon_ahead
+    ]
+    for copy in second:
+        copy.wait_recv()
     value = from_lon[0]
     for n in range(1, lons):
         value = value + from_lon[n]
-    lat_all[dp] = value
-    swap(3, "dp", dp_ahead, lambda peer: lat_all.at[dp], lat_all.at[dp])
-    total[lat] = lat_all[...]
-    swap(4, "lat", lat_ahead, lambda peer: lat_all, total.at[lat])
+    total[lat, dp] = value
+    third = [
+        put(total.at[lat, dp], total.at[lat, dp], send.at[1, d], recv.at[1, d],
+            {"lat": a, "dp": b})
+        for d, a, b in ahead
+    ]
+    for copy in third:
+        copy.wait_recv()
     for copy in sent:
         copy.wait_send()
 
@@ -473,7 +513,6 @@
     length = packed.shape[1]
     rows = -(-length // (128 * 8 * dps * lats)) * 8
     padded = jnp.pad(packed[0], (0, rows * 128 * dps * lats - length))
-    most = max(dps, lats, lons)
     f32 = jnp.float32
     piece = (rows, 128)
     total = pl.pallas_call(
@@ -483,12 +522,11 @@
         out_specs=pl.BlockSpec(memory_space=pltpu.VMEM),
         scratch_shapes=[
             pltpu.VMEM((lats, dps) + piece, f32),
-            pltpu.VMEM((dps,) + piece, f32),
-            pltpu.VMEM((dps,) + piece, f32),
             pltpu.VMEM((lons,) + piece, f32),
-            pltpu.VMEM((dps,) + piece, f32),
-            pltpu.SemaphoreType.DMA((5, most)),
-            pltpu.SemaphoreType.DMA((5, most)),
+            pltpu.SemaphoreType.DMA((2, dps * lats)),
+            pltpu.SemaphoreType.DMA((2, dps * lats)),
+            pltpu.SemaphoreType.DMA((lons,)),
+            pltpu.SemaphoreType.DMA((lons,)),
         ],
         compiler_params=pltpu.CompilerParams(collective_id=6, has_side_effects=True),
     )(padded.reshape((lats, dps) + piece))
@@ -509,30 +547,27 @@
     order = jnp.asarray(order_matrix(), bf)
     spread = jnp.asarray(spread_matrix(), bf)
     collect = jnp.asarray(spread_matrix().T.copy(), bf)
-    in_one, proj_one = fetch_first(w_qkv, w_out)
     in_two, proj_two = fetch_block(w_qkv, w_out, 1)
-    polar = lax.axis_index("lat") == lax.axis_size("lat") - 1
-    flag = jnp.where(polar, 1, 0).astype(jnp.int32).reshape(1)
     lines = jnp.pad(tables.reshape(2 * H, 1, RELS)[:, :, ::-1], ((0, 0), (0, 0), (0, TABLE - RELS)))
     field = ((ROWS, features), bf)
-    x_one, g_out, bias = call(
-        prep_kernel,
-        [field, field, ((2 * H, ROWS, ROWS), f32)],
+    bias = ((H, ROWS, ROWS), f32)
+    (in_one, proj_one), (x_one, g_out, bias_one, bias_two) = fetch_first(
+        w_qkv,
+        w_out,
+        (tokens[0], cotangent[0], lines, order, spread),
+        [field, field, bias, bias],
         [((LINES, LINE, features), bf), ((ROWS, SPAN), f32)],
-        (tokens[0], cotangent[0], lines, order, spread, flag),
-        smem=(5,),
-        flops=8 * 10**9,
     )
     saved = [((ROWS, 3 * inner), bf), ((H, ROWS, ROWS), bf)]
     wide = [((ROWS, inner), bf)]
     g_two = shift_quads(g_out, True)
     gain_one, gain_two = gains[0:1], gains[1:2]
     first, qkv_one, probs_one = call(
-        forward_kernel, [field] + saved, wide, (x_one, gain_one, in_one, proj_one, bias[:H])
+        forward_kernel, [field] + saved, wide, (x_one, gain_one, in_one, proj_one, bias_one)
     )
     x_two = exchange(first, True, 1)
     second, qkv_two, probs_two = call(
-        forward_kernel, [field] + saved, wide, (x_two, gain_two, in_two, proj_two, bias[H:])
+        forward_kernel, [field] + saved, wide, (x_two, gain_two, in_two, proj_two, bias_two)
     )
     y_back = shift_quads(second, False)
     back = [((ROWS, inner), bf), ((ROWS, 3 * inner), bf), ((H, ROWS, SPAN), f32)]

time: 183 us -> 171 us (0.934)
  Pallas kernels: 140 us -> 128 us
  local copies, waits for them, and re-layouts: 17 us -> 12.3 us
  starting transfers between devices: 7.85 us -> 11.5 us
    pallas_call x5 -> x4, Pallas kernels: 57.3 us -> 40.4 us  [call(): pl.pallas_call(kernel, out_shape=[jax.ShapeDtypeStruct(shape, dtype) for...]
    pallas_call x1, Pallas kernels: 32.9 us -> 40.8 us  [fetch_first(): pl.pallas_call(gather_kernel, out_shape=[jax.ShapeDtypeStruct(shape, dtyp...]
    slice x1 -> x0, local copies, waits for them, and re-layouts: 4.75 us -> none  [on_device(): bias[H:]]
    ppermute x6, starting transfers between devices: 7.77 us -> 11.4 us  [shift_quads(): arrived.append(lax.ppermute(quads[quad], ('lat', 'lon'), pairs))]
  transfers between devices with their start and end apart: 8 -> 8, of which waited for: 0 -> 0; matrix products, arithmetic and copies ran while one was open for 7% -> 5% of each run, Pallas kernels for 60% -> 59%
where the time goes in v3:
time: 171 us; the launch traced here: 170 us
  Pallas kernels  128 us (75%)
  between operations  14.2 us (8%)
  local copies, waits for them, and re-layouts  12.3 us (7%)
  starting transfers between devices  11.5 us (7%)
  other arithmetic  3.48 us (2%)
    pallas_call x1, Pallas kernels, fetch_first(): pl.pallas_call(gather_kernel, out_shape=[jax.ShapeDtypeStruct(shape, dtyp...  40.8 us
    pallas_call x4, Pallas kernels, call(): pl.pallas_call(kernel, out_shape=[jax.ShapeDtypeStruct(shape, dtype) for...  40.4 us
    pallas_call x2, Pallas kernels, exchange(): pl.pallas_call(functools.partial(exchange_kernel, ahead), out_shape=jax.S...  33.2 us
    pallas_call x1, Pallas kernels, sum_all(): pl.pallas_call(reduce_kernel, out_shape=jax.ShapeDtypeStruct((lats, dps)...  14 us
    ppermute x6, starting transfers between devices, shift_quads(): arrived.append(lax.ppermute(quads[quad], ('lat', 'lon'), pairs))  11.4 us
  transfers between devices with their start and end apart: 8, of which 0 were waited for; matrix products, arithmetic and copies ran while one was open for 5% of the time, Pallas kernels for 59%

profile of v3, /device:TPU:0, one launch (start us, length us, event | category | flops | bytes accessed | tf_op | source)
XLA Modules:
  0.0 170.0 jit_solution(13950273936463164972)
XLA Ops:
  7.2 0.0 copy-start.1
  7.2 0.0 all-gather.7.cloned.1.call-start
  7.2 1.6 slice.63
  8.8 0.0 all-gather.7.cloned.1.call-update
  8.8 0.0 all-gather.5.cloned.1.call-start
  8.9 1.8 %slice.62 = bf16[1,128,1536]{2,1,0:T(8,128)(2,1)} slice(bf16[2,128,1536]{2,1,0:T(8,128)(2,1)} %param.11), slice={[1:2], [0:128], [0:1536]} | slice | bytes 786432 | tf_op jit(solution)/shard_map/slice | solution.py:538
  10.6 0.0 all-gather.5.cloned.1.call-update
  10.7 1.0 reshape.73
  11.6 1.2 reverse
  12.8 0.2 slice.79
  13.1 0.7 pad.8.tab
  13.8 40.8 %shard_map.120 = (bf16[8,4,32,1536]{3,2,1,0:T(8,128)(2,1)}, bf16[8,4,16,1024]{3,2,1,0:T(8,128)(2,1)}, bf16[256,1024]{1,0:T(8,128)(2,1)}, bf16[256,1024]{1,0:T(8,...) custom-call(bf16[2,4,32,1536]{3,2,1,0:T(8,128)(2,1)} %bitcast.33, bf16[2,4,16,1024]{3,2,1,0:T(8,128)(2,1)} %bitcast.36, ...), custom_call_target="tpu_custom_call" | custom-call | tf_op jit(solution)/shard_map/pallas_call | solution.py:427
  54.6 1.1 fusion.1
  55.8 5.0 %collective-permute-start.2 = (bf16[64,1024]{1,0:T(8,128)(2,1)S(1)}, bf16[64,1024]{1,0:T(8,128)(2,1)S(1)}, u32[]{:S(2)}, u32[]{:S(2)}) collective-permute-start(bf16[64,1024]{1,0:T(8,128)(2,1)S(1)} %get-tuple-element.47), channel_id=1, source_target_pairs={{0,7},{1,4},{2,5},{3,6},{4,3},{5,0},{6,1},{7,2},{8,15},{9,12},{10,... | collective-permute-start | bytes 393224 | tf_op jit(solution)/shard_map/ppermute | solution.py:332
  60.7 3.0 %collective-permute-start.1 = (bf16[64,1024]{1,0:T(8,128)(2,1)S(1)}, bf16[64,1024]{1,0:T(8,128)(2,1)S(1)}, u32[]{:S(2)}, u32[]{:S(2)}) collective-permute-start(bf16[64,1024]{1,0:T(8,128)(2,1)S(1)} %get-tuple-element.48), channel_id=1, source_target_pairs={{0,4},{1,5},{2,6},{3,7},{4,0},{5,1},{6,2},{7,3},{8,12},{9,13},{10,... | collective-permute-start | bytes 393224 | tf_op jit(solution)/shard_map/ppermute | solution.py:332
  63.7 0.0 collective-permute-start
  63.7 0.0 copy-done.1
  63.7 0.6 fusion.2
  64.3 6.7 %shard_map.121 = (bf16[256,1024]{1,0:T(8,128)(2,1)}, bf16[256,1536]{1,0:T(8,128)(2,1)}, bf16[8,256,256]{2,1,0:T(8,128)(2,1)}) custom-call(bf16[256,1024]{1,0:T(8,128)(2,1)} %get-tuple-element.24.x_ref, f32[1,1024]{1,0:T(1,128)} %get-tuple-element.51.gain, bf16[1024,1536]{1,0:T(8,128)(2,1)} %bitcast.22, bf16[512,1024]{1,0:T(8,128)(2,1)} %bitcast.28, ...), custom_call_target="tpu_custom_call" | custom-call | flops 1000000000 | bytes 8388608 | tf_op jit(solution)/shard_map/pallas_call | solution.py:304
  71.1 21.3 %shard_map.122 = bf16[4,64,1024]{2,1,0:T(8,128)(2,1)} custom-call(bf16[4,64,1024]{2,1,0:T(8,128)(2,1)} %bitcast.38), custom_call_target="tpu_custom_call" | custom-call | tf_op jit(solution)/shard_map/pallas_call | solution.py:284
  92.4 0.0 all-gather.7.cloned.1.call-done
  92.4 0.0 all-gather.5.cloned.1.call-done
  92.5 6.7 %shard_map.123 = (bf16[256,1024]{1,0:T(8,128)(2,1)}, bf16[256,1536]{1,0:T(8,128)(2,1)}, bf16[8,256,256]{2,1,0:T(8,128)(2,1)}) custom-call(bf16[256,1024]{1,0:T(8,128)(2,1)} %bitcast.26, f32[1,1024]{1,0:T(1,128)} %get-tuple-element.50.gain, bf16[1024,1536]{1,0:T(8,128)(2,1)} %bitcast.24, bf16[512,1024]{1,0:T(8,128)(2,1)} %bitcast.30, ...), custom_call_target="tpu_custom_call" | custom-call | flops 1000000000 | bytes 8388608 | tf_op jit(solution)/shard_map/pallas_call | solution.py:304
  99.1 1.1 fusion
  100.3 2.1 %collective-permute-start.3 = (bf16[64,1024]{1,0:T(8,128)(2,1)S(1)}, bf16[64,1024]{1,0:T(8,128)(2,1)S(1)}, u32[]{:S(2)}, u32[]{:S(2)}) collective-permute-start(bf16[64,1024]{1,0:T(8,128)(2,1)S(1)} %get-tuple-element.42), channel_id=1, source_target_pairs={{0,5},{1,6},{2,7},{3,4},{4,1},{5,2},{6,3},{7,0},{8,13},{9,14},{10,... | collective-permute-start | bytes 393224 | tf_op jit(solution)/shard_map/ppermute | solution.py:332
  102.4 1.4 collective-permute-start.5
  103.7 0.0 collective-permute-done.2
  103.7 0.0 collective-permute-start.4
  103.7 0.0 collective-permute-done.1
  103.7 0.0 collective-permute-done
  103.8 0.8 pad_maximum_fusion.g_ref
  104.6 13.1 %shard_map.124 = (bf16[256,1024]{1,0:T(8,128)(2,1)}, f32[1,1024]{1,0:T(1,128)}, f32[8,1,1280]{2,1,0:T(1,128)}) custom-call(bf16[256,1024]{1,0:T(8,128)(2,1)} %pad_maximum_fusion.g_ref, bf16[256,1024]{1,0:T(8,128)(2,1)} %bitcast.27, f32[1,1024]{1,0:T(1,128)} %get-tuple-element.50.gain, bf16[1024,1536]{1,0:T(8,128)(2,1)} %bitcast.25, ...), custom_call_target="tpu_custom_call" | custom-call | flops 1000000000 | bytes 8388608 | tf_op jit(solution)/shard_map/pallas_call | solution.py:304
  117.7 11.8 %shard_map.125 = bf16[4,64,1024]{2,1,0:T(8,128)(2,1)} custom-call(bf16[4,64,1024]{2,1,0:T(8,128)(2,1)} %bitcast.37), custom_call_target="tpu_custom_call" | custom-call | tf_op jit(solution)/shard_map/pallas_call | solution.py:284
  129.6 0.0 collective-permute-done.3
  129.6 0.0 collective-permute-done.5
  129.6 0.0 collective-permute-done.4
  129.6 0.8 pad_maximum_fusion.1.y_ref
  130.4 0.0 copy-start
  130.4 0.0 copy-start.2
  130.4 13.9 %shard_map.126 = (bf16[3,6,12,1024]{3,2,1,0:T(8,128)(2,1)}, f32[1,1024]{1,0:T(1,128)}, f32[8,1,1280]{2,1,0:T(1,128)}, bf16[3,6,12,1024]{3,2,1,0:T(8,128)(2,1)}) custom-call(bf16[256,1024]{1,0:T(8,128)(2,1)} %bitcast.32, bf16[256,1024]{1,0:T(8,128)(2,1)} %get-tuple-element.24.x_ref, f32[1,1024]{1,0:T(1,128)} %get-tuple-element.51.gain, ...), custom_call_target="tpu_custom_call" | custom-call | flops 1000000000 | bytes 8388608 | tf_op jit(solution)/shard_map/pallas_call | solution.py:304
  144.3 0.0 copy-done
  144.3 0.0 copy-done.2
  144.3 0.9 pad_maximum_fusion.2
  145.1 0.7 pad.9
  145.8 14.0 %shard_map.127 = f32[2,4,24,128]{3,2,1,0:T(8,128)} custom-call(f32[2,4,24,128]{3,2,1,0:T(8,128)} %bitcast.39), custom_call_target="tpu_custom_call" | custom-call | tf_op jit(solution)/shard_map/pallas_call | solution.py:518
  159.8 1.0 slice_multiply_fusion
  160.8 0.2 slice_reduce_fusion
  161.1 0.7 reverse.1
  161.8 0.7 slice.80
  162.5 0.6 reshape.84
  (2 shorter events, 0.0 us)
Async XLA Ops:
  7.2 56.6 %copy-start.1 = (f32[2,1024]{1,0:T(2,128)S(1)}, f32[2,1024]{1,0:T(2,128)}, u32[]{:S(2)}) copy-start(f32[2,1024]{1,0:T(2,128)} %param.13) | copy-start | bytes 24580
  7.2 85.3 %all-gather.7.cloned.1.call-start = ((), (), s32[]{:S(2)}) async-start(), calls=%async_computation.1 | async-start | bytes 1179648 | tf_op jit(solution)/shard_map/all_gather | solution.py:539
  8.8 83.6 %all-gather.5.cloned.1.call-start = ((), (), s32[]{:S(2)}) async-start(), calls=%async_computation | async-start | bytes 3538944 | tf_op jit(solution)/shard_map/all_gather | solution.py:538
  55.8 48.0 %collective-permute-start.2 = (bf16[64,1024]{1,0:T(8,128)(2,1)S(1)}, bf16[64,1024]{1,0:T(8,128)(2,1)S(1)}, u32[]{:S(2)}, u32[]{:S(2)}) collective-permute-start(bf16[64,1024]{1,0:T(8,128)(2,1)S(1)} %get-tuple-element.47), channel_id=1, source_target_pairs={{0,7},{1,4},{2,5},{3,6},{4,3},{5,0},{6,1},{7,2},{8,15},{9,12},{10,... | collective-permute-start | bytes 393224 | tf_op jit(solution)/shard_map/ppermute | solution.py:332
  60.7 43.0 %collective-permute-start.1 = (bf16[64,1024]{1,0:T(8,128)(2,1)S(1)}, bf16[64,1024]{1,0:T(8,128)(2,1)S(1)}, u32[]{:S(2)}, u32[]{:S(2)}) collective-permute-start(bf16[64,1024]{1,0:T(8,128)(2,1)S(1)} %get-tuple-element.48), channel_id=1, source_target_pairs={{0,4},{1,5},{2,6},{3,7},{4,0},{5,1},{6,2},{7,3},{8,12},{9,13},{10,... | collective-permute-start | bytes 393224 | tf_op jit(solution)/shard_map/ppermute | solution.py:332
  63.7 40.0 %collective-permute-start = (bf16[64,1024]{1,0:T(8,128)(2,1)S(1)}, bf16[64,1024]{1,0:T(8,128)(2,1)S(1)}, u32[]{:S(2)}, u32[]{:S(2)}) collective-permute-start(bf16[64,1024]{1,0:T(8,128)(2,1)S(1)} %get-tuple-element.49), channel_id=1, source_target_pairs={{0,3},{1,0},{2,1},{3,2},{4,7},{5,4},{6,5},{7,6},{8,11},{9,8},{10,9... | collective-permute-start | bytes 393224 | tf_op jit(solution)/shard_map/ppermute | solution.py:332
  100.3 29.3 %collective-permute-start.3 = (bf16[64,1024]{1,0:T(8,128)(2,1)S(1)}, bf16[64,1024]{1,0:T(8,128)(2,1)S(1)}, u32[]{:S(2)}, u32[]{:S(2)}) collective-permute-start(bf16[64,1024]{1,0:T(8,128)(2,1)S(1)} %get-tuple-element.42), channel_id=1, source_target_pairs={{0,5},{1,6},{2,7},{3,4},{4,1},{5,2},{6,3},{7,0},{8,13},{9,14},{10,... | collective-permute-start | bytes 393224 | tf_op jit(solution)/shard_map/ppermute | solution.py:332
  102.4 27.2 %collective-permute-start.5 = (bf16[64,1024]{1,0:T(8,128)(2,1)S(1)}, bf16[64,1024]{1,0:T(8,128)(2,1)S(1)}, u32[]{:S(2)}, u32[]{:S(2)}) collective-permute-start(bf16[64,1024]{1,0:T(8,128)(2,1)S(1)} %get-tuple-element.44), channel_id=1, source_target_pairs={{0,1},{1,2},{2,3},{3,0},{4,5},{5,6},{6,7},{7,4},{8,9},{9,10},{10,1... | collective-permute-start | bytes 393224 | tf_op jit(solution)/shard_map/ppermute | solution.py:332
  103.7 25.9 %collective-permute-start.4 = (bf16[64,1024]{1,0:T(8,128)(2,1)S(1)}, bf16[64,1024]{1,0:T(8,128)(2,1)S(1)}, u32[]{:S(2)}, u32[]{:S(2)}) collective-permute-start(bf16[64,1024]{1,0:T(8,128)(2,1)S(1)} %get-tuple-element.45), channel_id=1, source_target_pairs={{0,4},{1,5},{2,6},{3,7},{4,0},{5,1},{6,2},{7,3},{8,12},{9,13},{10,... | collective-permute-start | bytes 393224 | tf_op jit(solution)/shard_map/ppermute | solution.py:332
  130.4 13.9 %copy-start = (f32[8,1,1280]{2,1,0:T(1,128)S(1)}, f32[8,1,1280]{2,1,0:T(1,128)}, u32[]{:S(2)}) copy-start(f32[8,1,1280]{2,1,0:T(1,128)} %get-tuple-element.41) | copy-start | bytes 122884
  130.4 13.9 %copy-start.2 = (f32[1,1024]{1,0:T(1,128)S(1)}, f32[1,1024]{1,0:T(1,128)}, u32[]{:S(2)}) copy-start(f32[1,1024]{1,0:T(1,128)} %get-tuple-element.39) | copy-start | bytes 12292
Sparse Core Ops, SparseCore 0:
  9.6 33.2 all-gather.6
  45.1 47.1 all-gather.4

commit v4 on v3

--- a/solution.py
+++ b/solution.py
@@ -237,26 +237,23 @@
             target[k // WH, k % WH] = lines[k * LINE : k * LINE + WW]
 
 
-def exchange_kernel(ahead, src, dst, send, recv, own):
+def quad_target(quad, ahead, sign):
     lat, lon = lax.axis_index("lat"), lax.axis_index("lon")
     lats, lons = lax.axis_size("lat"), lax.axis_size("lon")
-
-    def to(quad, sign):
-        y, x = quad // 2, quad % 2
-        if ahead:
-            dy, dx = 1 - y, 1 - x
-        else:
-            dy, dx = y, x
-        return {
-            "lat": lax.rem(lat + lats + sign * dy, lats),
-            "lon": lax.rem(lon + lons + sign * dx, lons),
-        }
-
+    y, x = quad // 2, quad % 2
+    dy, dx = (1 - y, 1 - x) if ahead else (y, x)
+    return {
+        "lat": lax.rem(lat + lats + sign * dy, lats),
+        "lon": lax.rem(lon + lons + sign * dx, lons),
+    }
+
+
+def exchange_kernel(ahead, src, dst, send, recv, own):
     sign = -1 if ahead else 1
     moving = [quad for quad in range(4) if quad != (3 if ahead else 0)]
     barrier = pltpu.get_barrier_semaphore()
     for quad in moving:
-        pl.semaphore_signal(barrier, inc=1, device_id=to(quad, -sign), device_id_type=MESH)
+        pl.semaphore_signal(barrier, inc=1, device_id=quad_target(quad, ahead, -sign), device_id_type=MESH)
     stay = 3 if ahead else 0
     local = pltpu.make_async_copy(src.at[stay], dst.at[3 - stay], own)
     local.start()
@@ -269,7 +266,7 @@
                 dst_ref=dst.at[3 - quad],
                 send_sem=send.at[n],
                 recv_sem=recv.at[n],
-                device_id=to(quad, sign),
+                device_id=quad_target(quad, ahead, sign),
                 device_id_type=MESH,
             )
         )
@@ -340,19 +337,9 @@
     return me, ahead, behind
 
 
-def greet(axes):
-    barrier = pltpu.get_barrier_semaphore()
-    count = 0
-    for axis in axes:
-        for _, peer in peers_of(axis)[1]:
-            pl.semaphore_signal(barrier, inc=1, device_id={axis: peer}, device_id_type=MESH)
-            count += 1
-    pl.semaphore_wait(barrier, count)
-
-
-def gather_kernel(w_in, w_proj, tok, cot, tab, order, spread, full_in, full_proj, x_out, g_out,
-                  bias_one, bias_two, lines, rows, send_z, recv_z, send_p, recv_p, send_c,
-                  recv_c, own):
+def gather_kernel(w_in, w_proj, tok, cot, tab, order, spread, in_one, in_two, proj_one, proj_two,
+                  x_out, g_two, bias_one, bias_two, g_out, lines, rows, send_z, recv_z, send_p,
+                  recv_p, send_c, recv_c, send_g, recv_g, own):
     prep = functools.partial(prep_stage, tok=tok, cot=cot, tab=tab, order=order, spread=spread,
                              x_out=x_out, g_out=g_out, bias_one=bias_one, bias_two=bias_two,
                              lines=lines, rows=rows)
@@ -360,9 +347,18 @@
     lat, lat_ahead, _ = peers_of("lat")
     lon, lon_ahead, lon_behind = peers_of("lon")
     lons = lax.axis_size("lon")
-    arrays = ((w_in, full_in), (w_proj, full_proj))
+    arrays = (
+        (w_in.at[0], in_one), (w_proj.at[0], proj_one),
+        (w_in.at[1], in_two), (w_proj.at[1], proj_two),
+    )
     mine = lat * lons + lon
-    greet(("dp", "lat", "lon"))
+    barrier = pltpu.get_barrier_semaphore()
+    friends = [{"dp": peer} for _, peer in dp_ahead] + [{"lat": peer} for _, peer in lat_ahead]
+    friends += [{"lon": peer} for _, peer in lon_ahead]
+    friends += [quad_target(quad, True, 1) for quad in range(3)]
+    for friend in friends:
+        pl.semaphore_signal(barrier, inc=1, device_id=friend, device_id_type=MESH)
+    pl.semaphore_wait(barrier, len(friends))
     sent = []
 
     def put(src, dst, send, recv, device):
@@ -377,17 +373,23 @@
     along = {}
     for d, peer in lon_ahead:
         for n, (part, full) in enumerate(arrays):
-            along[d, n] = put(part.at[0, dp], full.at[mine, dp], send_z.at[n, d], recv_z.at[n, d],
+            along[d, n] = put(part.at[dp], full.at[mine, dp], send_z.at[n, d], recv_z.at[n, d],
                               {"lon": peer})
     local = []
     across = []
     for n, (part, full) in enumerate(arrays):
-        local.append(pltpu.make_async_copy(part.at[0], full.at[mine], own.at[n]))
+        local.append(pltpu.make_async_copy(part, full.at[mine], own.at[n]))
         local[-1].start()
         for f, peer in lat_ahead:
-            across.append(put(part.at[0], full.at[mine], send_c.at[n, 0, f], recv_c.at[n, 0, f],
+            across.append(put(part, full.at[mine], send_c.at[n, 0, f], recv_c.at[n, 0, f],
                               {"lat": peer}))
     prep(0)
+    g_two[0:QR] = g_out[3 * QR : 4 * QR]
+    rolled = [
+        put(g_out.at[pl.ds(quad * QR, QR)], g_two.at[pl.ds((3 - quad) * QR, QR)], send_g.at[quad],
+            recv_g.at[quad], quad_target(quad, True, -1))
+        for quad in range(3)
+    ]
     plane = {}
     for d, source in lon_behind:
         shard = lat * lons + source
@@ -408,37 +410,43 @@
     prep(2)
     for copy in local:
         copy.wait()
-    for copy in across:
+    for copy in across + rolled:
         copy.wait_recv()
     for copy in sent:
         copy.wait_send()
 
 
-def fetch_first(w_qkv, w_out, prep_args, prep_out, prep_scratch):
+def fetch_all(w_qkv, w_out, prep_args, prep_out, prep_scratch):
     dps, lats, lons = (lax.axis_size(axis) for axis in ("dp", "lat", "lon"))
     shards = lats * lons
     if w_qkv.shape[1] % (16 * dps) or w_out.shape[1] % (16 * dps):
-        full = fetch_block(w_qkv, w_out, 0)
-        return full, call(prep_kernel, prep_out, prep_scratch, prep_args, flops=8 * 10**9)
+        one, two = fetch_block(w_qkv, w_out, 0), fetch_block(w_qkv, w_out, 1)
+        x_one, g_out, bias_one, bias_two = call(
+            prep_kernel, prep_out, prep_scratch, prep_args, flops=8 * 10**9
+        )
+        return (one[0], two[0], one[1], two[1]), (
+            x_one, shift_quads(g_out, True), bias_one, bias_two
+        )
     parts = [w.reshape(2, dps, w.shape[1] // dps, w.shape[2]) for w in (w_qkv, w_out)]
     dma = pltpu.SemaphoreType.DMA
-    shapes = [((shards,) + part.shape[1:], part.dtype) for part in parts] + prep_out
+    shapes = [((shards,) + part.shape[1:], part.dtype) for part in parts for _ in range(2)]
     vmem = pl.BlockSpec(memory_space=pltpu.VMEM)
+    shapes = shapes + prep_out
     found = pl.pallas_call(
         gather_kernel,
         out_shape=[jax.ShapeDtypeStruct(shape, dtype) for shape, dtype in shapes],
         in_specs=[vmem] * (2 + len(prep_args)),
         out_specs=[vmem] * len(shapes),
-        scratch_shapes=[pltpu.VMEM(shape, dtype) for shape, dtype in prep_scratch]
+        scratch_shapes=[pltpu.VMEM(shape, dtype) for shape, dtype in prep_out[1:2] + prep_scratch]
         + [
-            dma((2, lons)), dma((2, lons)), dma((2, lons, dps)), dma((2, lons, dps)),
-            dma((2, lons, lats)), dma((2, lons, lats)), dma((2,)),
+            dma((4, lons)), dma((4, lons)), dma((4, lons, dps)), dma((4, lons, dps)),
+            dma((4, lons, lats)), dma((4, lons, lats)), dma((3,)), dma((3,)), dma((4,)),
         ],
         compiler_params=pltpu.CompilerParams(
             collective_id=5, has_side_effects=True, vmem_limit_bytes=VMEM_LIMIT
         ),
     )(*parts, *prep_args)
-    return tuple(array.reshape(-1, array.shape[-1]) for array in found[:2]), found[2:]
+    return tuple(array.reshape(-1, array.shape[-1]) for array in found[:4]), found[4:]
 
 
 def plane_peers():
@@ -547,11 +555,10 @@
     order = jnp.asarray(order_matrix(), bf)
     spread = jnp.asarray(spread_matrix(), bf)
     collect = jnp.asarray(spread_matrix().T.copy(), bf)
-    in_two, proj_two = fetch_block(w_qkv, w_out, 1)
     lines = jnp.pad(tables.reshape(2 * H, 1, RELS)[:, :, ::-1], ((0, 0), (0, 0), (0, TABLE - RELS)))
     field = ((ROWS, features), bf)
     bias = ((H, ROWS, ROWS), f32)
-    (in_one, proj_one), (x_one, g_out, bias_one, bias_two) = fetch_first(
+    (in_one, in_two, proj_one, proj_two), (x_one, g_two, bias_one, bias_two) = fetch_all(
         w_qkv,
         w_out,
         (tokens[0], cotangent[0], lines, order, spread),
@@ -560,7 +567,6 @@
     )
     saved = [((ROWS, 3 * inner), bf), ((H, ROWS, ROWS), bf)]
     wide = [((ROWS, inner), bf)]
-    g_two = shift_quads(g_out, True)
     gain_one, gain_two = gains[0:1], gains[1:2]
     first, qkv_one, probs_one = call(
         forward_kernel, [field] + saved, wide, (x_one, gain_one, in_one, proj_one, bias_one)

time: 171 us -> 159 us (0.930)
  Pallas kernels: 128 us -> 144 us
  between operations: 14.2 us -> 0.75 us
  starting transfers between devices: 11.5 us -> 1.86 us
  local copies, waits for them, and re-layouts: 12.3 us -> 8.57 us
    pallas_call x1, Pallas kernels: 40.8 us -> 59.8 us  [fetch_all(): pl.pallas_call(gather_kernel, out_shape=[jax.ShapeDtypeStruct(shape, dtyp...]
    ppermute x6 -> x3, starting transfers between devices: 11.4 us -> 1.86 us  [shift_quads(): arrived.append(lax.ppermute(quads[quad], ('lat', 'lon'), pairs))]
    slice x3 -> x0, local copies, waits for them, and re-layouts: 4.48 us -> none  [the longest x1 1.77 us: fetch_block(): w_qkv[index]]
    pallas_call x2, Pallas kernels: 33.2 us -> 30.2 us  [exchange(): pl.pallas_call(functools.partial(exchange_kernel, ahead), out_shape=jax.S...]
  transfers between devices with their start and end apart: 8 -> 3, of which waited for: 0 -> 0; matrix products, arithmetic and copies ran while one was open for 5% -> 0% of each run, Pallas kernels for 59% -> 16%
where the time goes in v4:
time: 159 us; the launch traced here: 158 us
  Pallas kernels  144 us (91%)
  local copies, waits for them, and re-layouts  8.57 us (5%)
  other arithmetic  2.67 us (2%)
  starting transfers between devices  1.86 us (1%)
    pallas_call x1, Pallas kernels, fetch_all(): pl.pallas_call(gather_kernel, out_shape=[jax.ShapeDtypeStruct(shape, dtyp...  59.8 us
    pallas_call x4, Pallas kernels, call(): pl.pallas_call(kernel, out_shape=[jax.ShapeDtypeStruct(shape, dtype) for...  40.3 us
    pallas_call x2, Pallas kernels, exchange(): pl.pallas_call(functools.partial(exchange_kernel, ahead), out_shape=jax.S...  30.2 us
    pallas_call x1, Pallas kernels, sum_all(): pl.pallas_call(reduce_kernel, out_shape=jax.ShapeDtypeStruct((lats, dps)...  14 us
  transfers between devices with their start and end apart: 3, of which 0 were waited for; matrix products, arithmetic and copies ran while one was open for 0% of the time, Pallas kernels for 16%

profile of v4, /device:TPU:0, one launch (start us, length us, event | category | flops | bytes accessed | tf_op | source)
XLA Modules:
  0.0 158.2 jit_solution(12793030487384479778)
XLA Ops:
  0.6 1.4 fusion.1
  2.0 1.0 reshape.70
  3.0 1.2 reverse
  4.2 0.2 slice.51
  4.4 0.7 pad.8.tab
  5.1 59.8 %shard_map.120 = (bf16[8,4,32,1536]{3,2,1,0:T(8,128)(2,1)}, bf16[8,4,32,1536]{3,2,1,0:T(8,128)(2,1)}, bf16[8,4,16,1024]{3,2,1,0:T(8,128)(2,1)}, bf16[8,4,16,1024...) custom-call(bf16[2,4,32,1536]{3,2,1,0:T(8,128)(2,1)} %bitcast.33, ...), custom_call_target="tpu_custom_call" | custom-call | tf_op jit(solution)/shard_map/pallas_call | solution.py:435
  65.0 6.6 %shard_map.121 = (bf16[256,1024]{1,0:T(8,128)(2,1)}, bf16[256,1536]{1,0:T(8,128)(2,1)}, bf16[8,256,256]{2,1,0:T(8,128)(2,1)}) custom-call(bf16[256,1024]{1,0:T(8,128)(2,1)} %get-tuple-element.26.x_ref, f32[1,1024]{1,0:T(1,128)} %get-tuple-element.51.gain, bf16[1024,1536]{1,0:T(8,128)(2,1)} %bitcast.22, bf16[512,1024]{1,0:T(8,128)(2,1)} %bitcast.28, ...), custom_call_target="tpu_custom_call" | custom-call | flops 1000000000 | bytes 8388608 | tf_op jit(solution)/shard_map/pallas_call | solution.py:301
  71.6 18.3 %shard_map.122 = bf16[4,64,1024]{2,1,0:T(8,128)(2,1)} custom-call(bf16[4,64,1024]{2,1,0:T(8,128)(2,1)} %bitcast.37), custom_call_target="tpu_custom_call" | custom-call | tf_op jit(solution)/shard_map/pallas_call | solution.py:281
  89.9 6.7 %shard_map.123 = (bf16[256,1024]{1,0:T(8,128)(2,1)}, bf16[256,1536]{1,0:T(8,128)(2,1)}, bf16[8,256,256]{2,1,0:T(8,128)(2,1)}) custom-call(bf16[256,1024]{1,0:T(8,128)(2,1)} %bitcast.26, f32[1,1024]{1,0:T(1,128)} %get-tuple-element.50.gain, bf16[1024,1536]{1,0:T(8,128)(2,1)} %bitcast.24, bf16[512,1024]{1,0:T(8,128)(2,1)} %bitcast.30, ...), custom_call_target="tpu_custom_call" | custom-call | flops 1000000000 | bytes 8388608 | tf_op jit(solution)/shard_map/pallas_call | solution.py:301
  96.6 1.1 fusion
  97.7 0.1 collective-permute-start
  97.8 1.4 collective-permute-start.2
  99.1 0.4 collective-permute-start.1
  99.6 13.1 %shard_map.124 = (bf16[256,1024]{1,0:T(8,128)(2,1)}, f32[1,1024]{1,0:T(1,128)}, f32[8,1,1280]{2,1,0:T(1,128)}) custom-call(bf16[256,1024]{1,0:T(8,128)(2,1)} %get-tuple-element.25.g_ref, bf16[256,1024]{1,0:T(8,128)(2,1)} %bitcast.27, f32[1,1024]{1,0:T(1,128)} %get-tuple-element.50.gain, bf16[1024,1536]{1,0:T(8,128)(2,1)} %bitcast.25, ...), custom_call_target="tpu_custom_call" | custom-call | flops 1000000000 | bytes 8388608 | tf_op jit(solution)/shard_map/pallas_call | solution.py:301
  112.7 11.9 %shard_map.125 = bf16[4,64,1024]{2,1,0:T(8,128)(2,1)} custom-call(bf16[4,64,1024]{2,1,0:T(8,128)(2,1)} %bitcast.36), custom_call_target="tpu_custom_call" | custom-call | tf_op jit(solution)/shard_map/pallas_call | solution.py:281
  124.6 0.0 collective-permute-done
  124.6 0.0 collective-permute-done.2
  124.6 0.0 collective-permute-done.1
  124.6 0.8 pad_maximum_fusion.y_ref
  125.5 0.0 copy-start
  125.5 0.0 copy-start.1
  125.5 13.9 %shard_map.126 = (bf16[3,6,12,1024]{3,2,1,0:T(8,128)(2,1)}, f32[1,1024]{1,0:T(1,128)}, f32[8,1,1280]{2,1,0:T(1,128)}, bf16[3,6,12,1024]{3,2,1,0:T(8,128)(2,1)}) custom-call(bf16[256,1024]{1,0:T(8,128)(2,1)} %bitcast.32, bf16[256,1024]{1,0:T(8,128)(2,1)} %get-tuple-element.26.x_ref, f32[1,1024]{1,0:T(1,128)} %get-tuple-element.51.gain, ...), custom_call_target="tpu_custom_call" | custom-call | flops 1000000000 | bytes 8388608 | tf_op jit(solution)/shard_map/pallas_call | solution.py:301
  139.3 0.0 copy-done
  139.3 0.0 copy-done.1
  139.3 0.9 pad_maximum_fusion.1
  140.2 0.6 pad.9
  140.9 14.0 %shard_map.127 = f32[2,4,24,128]{3,2,1,0:T(8,128)} custom-call(f32[2,4,24,128]{3,2,1,0:T(8,128)} %bitcast.38), custom_call_target="tpu_custom_call" | custom-call | tf_op jit(solution)/shard_map/pallas_call | solution.py:526
  154.9 1.0 slice_multiply_fusion
  155.9 0.2 slice_reduce_fusion
  156.1 0.7 reverse.1
  156.8 0.7 slice.52
  157.6 0.6 reshape.83
  (2 shorter events, 0.0 us)
Async XLA Ops:
  97.7 26.9 %collective-permute-start = (bf16[64,1024]{1,0:T(8,128)(2,1)S(1)}, bf16[64,1024]{1,0:T(8,128)(2,1)S(1)}, u32[]{:S(2)}, u32[]{:S(2)}) collective-permute-start(bf16[64,1024]{1,0:T(8,128)(2,1)S(1)} %get-tuple-element.46), channel_id=1, source_target_pairs={{0,5},{1,6},{2,7},{3,4},{4,1},{5,2},{6,3},{7,0},{8,13},{9,14},{10,... | collective-permute-start | bytes 393224 | tf_op jit(solution)/shard_map/ppermute | solution.py:329
  97.8 26.8 %collective-permute-start.2 = (bf16[64,1024]{1,0:T(8,128)(2,1)S(1)}, bf16[64,1024]{1,0:T(8,128)(2,1)S(1)}, u32[]{:S(2)}, u32[]{:S(2)}) collective-permute-start(bf16[64,1024]{1,0:T(8,128)(2,1)S(1)} %get-tuple-element.48), channel_id=1, source_target_pairs={{0,1},{1,2},{2,3},{3,0},{4,5},{5,6},{6,7},{7,4},{8,9},{9,10},{10,1... | collective-permute-start | bytes 393224 | tf_op jit(solution)/shard_map/ppermute | solution.py:329
  99.1 25.5 %collective-permute-start.1 = (bf16[64,1024]{1,0:T(8,128)(2,1)S(1)}, bf16[64,1024]{1,0:T(8,128)(2,1)S(1)}, u32[]{:S(2)}, u32[]{:S(2)}) collective-permute-start(bf16[64,1024]{1,0:T(8,128)(2,1)S(1)} %get-tuple-element.49), channel_id=1, source_target_pairs={{0,4},{1,5},{2,6},{3,7},{4,0},{5,1},{6,2},{7,3},{8,12},{9,13},{10,... | collective-permute-start | bytes 393224 | tf_op jit(solution)/shard_map/ppermute | solution.py:329
  125.5 13.9 %copy-start = (f32[8,1,1280]{2,1,0:T(1,128)S(1)}, f32[8,1,1280]{2,1,0:T(1,128)}, u32[]{:S(2)}) copy-start(f32[8,1,1280]{2,1,0:T(1,128)} %get-tuple-element.45) | copy-start | bytes 122884
  125.5 13.9 %copy-start.1 = (f32[1,1024]{1,0:T(1,128)S(1)}, f32[1,1024]{1,0:T(1,128)}, u32[]{:S(2)}) copy-start(f32[1,1024]{1,0:T(1,128)} %get-tuple-element.43) | copy-start | bytes 12292
